TPU v7x, 128 devices: a whole 4x4x4 slice. The times are simulated.
128 devices in a mesh: dom: 8 (over y, core), sub: 16 (over x, z).
Axes of the slice: x: 4, y: 4, z: 4, core: 2. Of those that a mesh axis runs over, the one named last changes fastest.
Arguments:
- adjoint_traces: bfloat16 [144, 1048576], P(None, ('dom', 'sub')), may hold values from -6 to 6
- primal_traces: bfloat16 [144, 1048576], P(None, ('dom', 'sub')), may hold values from -6 to 6
- jacobian: float32 [1048576], P(('dom', 'sub')), may hold values from 0.4 to 2.5
- stiffness: float32 [1048576], P(('dom', 'sub')), as said below
- connect: int32 [4, 1048576], P(None, ('dom', 'sub')), may hold values from 0 to 2047
- shared_perm: int32 [8, 16, 256], P('dom', 'sub'), may hold values from 0 to 255, each once within a row
- wall_owner: int32 [262144, 1], P(('dom', 'sub')), may hold values from 0 to 127; in each aligned block of 2048 rows (0 to 2047, 2048 to 4095, ...) at most 40 rows name the same one
- wall_patch: int32 [262144], P(('dom', 'sub')), may hold values from 0 to 15
- w_trace: bfloat16 [144, 384], replicated, may hold values from -0.5 to 0.5
- w_state: bfloat16 [144, 384], replicated, may hold values from -0.5 to 0.5
- w_node: bfloat16 [384, 12], replicated, may hold values from -1.25 to 1.25
- w_block: bfloat16 [384, 128], replicated, may hold values from -0.3125 to 0.3125
- w_adjoint: bfloat16 [12, 128], replicated, may hold values from -1.75 to 1.75
- stiff_ref: float32 [12, 12], replicated, as said below
Outputs:
- patch_grad: float32 [2048, 128], P(('dom', 'sub'))
- node_adjoint: float32 [3, 262144], P(None, ('dom', 'sub'))
Inputs may be any that keep to these rules, and one draw needn't show every extreme that they name: `shared_perm`: each partition's row is a permutation. `wall_owner`: among the 2048 wall elements of one partition no owner is named more than 40 times, a bound that some block reaches. `stiffness`: each entry lies between 0.15 and 6. `stiff_ref`: symmetric; each diagonal entry exceeds the sum of magnitudes of the other entries of its row.
All inputs are finite; a program needn't handle non-finite values.
Results may differ from a plain program's by a relative error of at most 0.0029.
Values sent between devices are 32-bit elements; how exact they have to be, the bound alone decides.
No kernel may reach another device: no remote copies, remote signals or barrier semaphores. Data moves between devices by JAX's collectives and lax.ppermute only.
A program may use at most 64 MiB of HBM per device.

v0:
```python
import jax
import jax.numpy as jnp
from jax import lax
from jax.sharding import PartitionSpec as P

PATCH_DEV = 16


mass_shift = 0.5
relax = 0.7


def passed_along(x, axis, by):
    devices = lax.axis_size(axis)
    pairs = [(i, i + by) for i in range(devices) if 0 <= i + by < devices]
    return lax.ppermute(x, axis, pairs)


def element_front(traces, states, jac_part, w_trace, w_state, w_node):
    upsilon = jnp.dot(w_trace.T, traces, preferred_element_type=jnp.float32)
    tangent = jnp.dot(w_state.T, states, preferred_element_type=jnp.float32)
    product = (jac_part[None, :] * upsilon * tangent).astype(jnp.bfloat16)
    node_terms = jnp.dot(w_node.T, product, preferred_element_type=jnp.float32)
    return (node_terms, product)


def assemble(values, conn_part, node_count):
    fields = values.shape[0] // 4
    flat_values = values.reshape(fields, -1)
    return (
        jnp.zeros((fields, node_count), jnp.float32).at[:, conn_part.reshape(-1)].add(flat_values)
    )


def at_elements(node_field, conn_part):
    fields = node_field.shape[0]
    return node_field[:, conn_part.reshape(-1)].reshape(fields * 4, -1)


def share_rims(node_field, rim_order):
    node_count = node_field.shape[1]
    rim_width = rim_order.shape[0]
    upper_rim = node_field[:, node_count - rim_width :]
    lower_rim = node_field[:, :rim_width]
    perm_table = (jnp.arange(rim_width, dtype=jnp.int32)[:, None] == rim_order[None, :]).astype(
        jnp.float32
    )
    lower_perm = jnp.dot(lower_rim, perm_table, precision=lax.Precision.HIGHEST)
    arrived = passed_along(upper_rim, "sub", 1)
    summed = lower_perm + arrived
    returned = passed_along(summed, "sub", -1)
    at_top = lax.axis_index("sub") == lax.axis_size("sub") - 1
    new_upper = jnp.where(at_top, upper_rim, returned)
    new_lower = jnp.dot(summed, perm_table.T, precision=lax.Precision.HIGHEST)
    return jnp.concatenate(
        [new_lower, node_field[:, rim_width : node_count - rim_width], new_upper], axis=1
    )


def per_device(
    adjoint_traces,
    primal_traces,
    jacobian,
    stiffness,
    connect,
    shared_perm,
    wall_owner,
    wall_patch,
    w_trace,
    w_state,
    w_node,
    w_block,
    w_adjoint,
    stiff_ref,
):
    elements = adjoint_traces.shape[1]
    wall_count = wall_owner.shape[0]
    node_total = elements // 4
    rim_order = shared_perm.reshape(-1)

    def front(start):
        return element_front(
            lax.dynamic_slice_in_dim(adjoint_traces, start, wall_count, 1),
            lax.dynamic_slice_in_dim(primal_traces, start, wall_count, 1),
            lax.dynamic_slice_in_dim(jacobian, start, wall_count, 0),
            w_trace,
            w_state,
            w_node,
        )

    wall_terms, wall_product = front(0)

    def later_block(block_id):
        return front((block_id + 1) * wall_count)[0]

    later_terms = lax.map(later_block, jnp.arange(elements // wall_count - 1, dtype=jnp.int32))
    node_terms = jnp.concatenate(
        [wall_terms, jnp.moveaxis(later_terms, 0, 1).reshape(12, elements - wall_count)], axis=1
    )
    ref_diag = jnp.diagonal(stiff_ref)
    both_terms = jnp.concatenate([node_terms, stiffness[None, :] * ref_diag[:, None]], axis=0)
    stacked = assemble(both_terms, connect, node_total)
    shared = share_rims(stacked, rim_order)
    sens_sum = shared[:3]
    diagonal = mass_shift + shared[3:]
    psi_one = relax * sens_sum / diagonal
    element_vals = at_elements(psi_one, connect)
    pushed = stiffness[None, :] * jnp.dot(stiff_ref, element_vals, precision=lax.Precision.HIGHEST)
    applied = share_rims(assemble(pushed, connect, node_total), rim_order)
    node_adjoint = psi_one + relax * (sens_sum - (mass_shift * psi_one + applied)) / diagonal
    psi_wall = at_elements(node_adjoint, connect[:, :wall_count])
    blocks = jnp.dot(wall_product.T, w_block, preferred_element_type=jnp.float32)
    blocks = blocks + jnp.dot(
        psi_wall.T, w_adjoint.astype(jnp.float32), precision=lax.Precision.HIGHEST
    )
    block_width = blocks.shape[1]
    dom_count = lax.axis_size("dom")
    sub_count = lax.axis_size("sub")
    devices = dom_count * sub_count
    capacity = wall_count // devices * 5 // 2
    owners = wall_owner.reshape(-1)
    owner_hits = (owners[:, None] == jnp.arange(devices, dtype=jnp.int32)[None, :]).astype(
        jnp.int32
    )
    running = jnp.cumsum(owner_hits, axis=0) - owner_hits
    slot_rank = jnp.sum(running * owner_hits, axis=1)
    slot_index = owners * capacity + slot_rank
    payload = jnp.zeros((devices * capacity, block_width), jnp.float32).at[slot_index].set(blocks)
    labels = (
        jnp.full((devices * capacity,), -1.0, jnp.float32)
        .at[slot_index]
        .set(wall_patch.astype(jnp.float32))
    )
    got_blocks, got_labels = (
        lax.all_to_all(
            payload.reshape(devices, capacity, block_width),
            ("dom", "sub"),
            split_axis=0,
            concat_axis=0,
            tiled=True,
        ),
        lax.all_to_all(
            labels.reshape(devices, capacity),
            ("dom", "sub"),
            split_axis=0,
            concat_axis=0,
            tiled=True,
        ),
    )
    selector = (
        got_labels.reshape(1, -1) == jnp.arange(PATCH_DEV, dtype=jnp.float32)[:, None]
    ).astype(jnp.float32)
    patch_grad = jnp.dot(
        selector, got_blocks.reshape(-1, block_width), precision=lax.Precision.HIGHEST
    )
    return (patch_grad, node_adjoint)


def solution(mesh):
    return jax.shard_map(
        per_device,
        mesh=mesh,
        in_specs=(
            P(None, ("dom", "sub")),
            P(None, ("dom", "sub")),
            P(("dom", "sub")),
            P(("dom", "sub")),
            P(None, ("dom", "sub")),
            P("dom", "sub", None),
            P(("dom", "sub"), None),
            P(("dom", "sub")),
            P(),
            P(),
            P(),
            P(),
            P(),
            P(),
        ),
        out_specs=(P(("dom", "sub"), None), P(None, ("dom", "sub"))),
        check_vma=False,
    )
```

profile of v0, /device:TPU:1, one launch (start us, length us, event | category | flops | bytes accessed | tf_op | source)
XLA Modules:
  0.0 645.0 jit_solution(9906468996105592223)
XLA Ops:
  3.3 3.4 fusion.18
  6.7 19.9 %while.10 = (s32[]{:T(128)}, f32[3,12,2048]{2,1,0:T(8,128)}, s32[3]{0:T(128)S(1)}, f32[8192]{0:T(1024)}, bf16[144,8192]{1,0:T(8,128)(2,1)}, /*index=5*/bf16[144,...) while((s32[]{:T(128)}, f32[3,12,2048]{2,1,0:T(8,128)}, ...), condition=%wide.region_5.6_spmd, body=%wide.region_4.5_spmd.sunk | while | flops 474218496 | bytes 7857379 | solution.py:96
  8.0 1.8 fusion.69
  10.5 2.9 fusion.70
  14.6 1.8 fusion.69
  17.2 2.8 fusion.70
  21.3 1.8 fusion.69
  23.8 2.8 fusion.70
  28.2 2.7 multiply_convert_fusion.1
  32.5 9.0 %copy.63 = f32[32768,6]{1,0:T(8,128)} copy(f32[32768,6]{0,1:T(8,128)S(1)} %bitcast.81) | data formatting | bytes 1572864 | tf_op jit(solution)/shard_map/reshape | solution.py:29
  41.6 174.4 %scatter_custom_fusion.1 = f32[6,2048]{0,1:T(8,128)S(1)} fusion(s32[32768]{0:T(1024)} %bitcast.84, f32[32768,6]{1,0:T(8,128)} %copy.63, f32[]{:T(128)} %constant.19.clone.1), kind=kCustom, calls=%fused_computation.39 | custom fusion | flops 196608 | bytes 49664 | tf_op jit(solution)/shard_map/scatter-add | solution.py:31
  216.8 5.0 collective-permute-start
  224.6 8.8 %scatter_custom_fusion = f32[5120]{0:T(1024)} fusion(s32[2048]{0:T(1024)} %bitcast.96, f32[2048]{0:T(1024)S(1)} %convert_element_type.23, f32[]{:T(128)} %constant.22.clone.1), kind=kCustom, calls=%fused_computation.69 | custom fusion | bytes 20992 | tf_op jit(solution)/shard_map/scatter | solution.py:132
  233.4 1.4 all_to_all.9
  234.9 10.4 %all-to-all-start = ((f32[128,1,40]{2,1,0:T(1,128)}), f32[128,1,40]{2,1,0:T(1,128)}, u32[]{:S(2)}, u32[]{:S(2)}) async-start(f32[128,1,40]{2,1,0:T(1,128)} %bitcast.89), calls=%async_computation | async-start | bytes 131072 | tf_op jit(solution)/shard_map/all_to_all | solution.py:142
  245.2 1.6 broadcast_clamp_fusion
  248.3 1.6 fusion.40
  251.1 1.5 collective-permute-start.1
  252.8 2.8 collective-permute-done.1
  256.0 108.5 %gather_fusion.1 = f32[32768,3]{1,0:T(8,128)} fusion(f32[3,2048]{0,1:T(8,128)S(1)} %copy.66, s32[32768]{0:T(1024)S(1)} %copy-done.8), kind=kCustom, calls=%fused_computation.1 | custom fusion | bytes 917504 | tf_op jit(solution)/shard_map/gather | solution.py:37
  364.4 9.5 %copy.67 = f32[3,32768]{1,0:T(4,128)S(1)} copy(f32[3,32768]{0,1:T(8,128)} %bitcast.78) | data formatting | bytes 786432 | tf_op jit(solution)/shard_map/gather | solution.py:37
  375.1 8.6 %copy.68 = f32[3,32768]{0,1:T(8,128)} copy(f32[3,32768]{1,0:T(4,128)S(1)} %reshape.172) | data formatting | bytes 786432 | tf_op jit(solution)/shard_map/reshape | solution.py:29
  383.7 158.6 %scatter_custom_fusion.2 = f32[3,2048]{0,1:T(8,128)S(1)} fusion(s32[32768]{0:T(1024)} %bitcast.86, f32[3,32768]{0,1:T(8,128)} %copy.68, f32[]{:T(128)} %constant.19.clone.1), kind=kCustom, calls=%fused_computation.15 | custom fusion | flops 98304 | bytes 16802304 | tf_op jit(solution)/shard_map/scatter-add | solution.py:31
  542.4 3.4 collective-permute-start.2
  548.2 3.1 collective-permute-done.3
  551.8 27.8 %gather_fusion.2 = f32[8192,3]{1,0:T(8,128)} fusion(f32[3,2048]{0,1:T(8,128)S(1)} %copy.71, s32[8192]{0:T(1024)S(1)} %broadcast_clamp_fusion.1), kind=kCustom, calls=%fused_computation.2 | custom fusion | bytes 229376 | tf_op jit(solution)/shard_map/gather | solution.py:37
  579.5 2.8 copy.72
  583.5 7.4 %scatter_custom_fusion.3 = f32[5120,128]{1,0:T(8,128)} fusion(s32[2048]{0:T(1024)} %bitcast.97, f32[2048,128]{1,0:T(8,128)S(1)} %convolution_add_fusion, f32[]{:T(128)} %constant.19.clone.1), kind=kCustom, calls=%fused_computation.22 | custom fusion | bytes 2621952 | tf_op jit(solution)/shard_map/scatter | solution.py:128
  590.8 17.3 %all-to-all-start.1 = ((f32[128,40,128]{2,1,0:T(8,128)}), f32[128,40,128]{2,1,0:T(8,128)S(1)}, u32[]{:S(2)}, u32[]{:S(2)}) async-start(f32[128,40,128]{2,1,0:T(8,128)} %bitcast.22), calls=%async_computation.1 | async-start | bytes 5242880 | tf_op jit(solution)/shard_map/all_to_all | solution.py:135
  608.7 1.6 reduce.3
  610.4 32.9 %all-to-all-done.1 = f32[128,40,128]{2,1,0:T(8,128)S(1)} async-done(((f32[128,40,128]{2,1,0:T(8,128)}), f32[128,40,128]{2,1,0:T(8,128)S(1)}, u32[]{:S(2)}, u32[]{:S(2)}) %all-to-all-start.1) | async-done | bytes 2621472 | tf_op jit(solution)/shard_map/all_to_all | solution.py:135
  643.4 1.6 fusion.24
  (97 shorter events, 22.2 us)
Async XLA Ops:
  0.6 247.6 %copy-start = (bf16[384,128]{1,0:T(8,128)(2,1)S(1)}, bf16[384,128]{1,0:T(8,128)(2,1)}, u32[]{:S(2)}) copy-start(bf16[384,128]{1,0:T(8,128)(2,1)} %param.27) | copy-start | bytes 294916
  0.6 6.1 copy-start.6
  0.7 6.1 copy-start.7
  0.7 6.1 copy-start.9
  28.2 3.1 copy-start.2
  28.2 3.8 copy-start.10
  32.5 189.3 %copy-start.13 = (s32[2048,1]{0,1:T(1,128)S(1)}, s32[2048,1]{0,1:T(1,128)}, u32[]{:S(2)}) copy-start(s32[2048,1]{0,1:T(1,128)} %param.22) | copy-start | bytes 24580
  216.0 5.8 copy-start.3
  216.8 33.3 %collective-permute-start = (f32[6,256]{1,0:T(8,128)}, f32[6,256]{1,0:T(8,128)}, u32[]{:S(2)}, u32[]{:S(2)}) collective-permute-start(f32[6,256]{1,0:T(8,128)} %copy.73), channel_id=1, source_target_pairs={{0,1},{1,2},{2,3},{3,4},{4,5},{5,6},{6,7},{7,8},{8,9},{9,10},{10,1... | collective-permute-start | bytes 18440 | tf_op jit(solution)/shard_map/ppermute | solution.py:16
  222.7 27.2 %slice-start = ((f32[6,2048]{0,1:T(8,128)}), f32[6,1536]{0,1:T(8,128)S(1)}, s32[]{:S(2)}) async-start(f32[6,2048]{0,1:T(8,128)} %copy-done.3), calls=%async_computation.2 | async-start | bytes 1572864 | tf_op jit(solution)/shard_map/slice | solution.py:56
  223.3 26.8 %copy-start.4 = (f32[6,2048]{0,1:T(8,128)S(1)}, f32[6,2048]{0,1:T(8,128)}, u32[]{:S(2)}) copy-start(f32[6,2048]{0,1:T(8,128)} %copy-done.3) | copy-start | bytes 147460
  233.4 16.7 %copy-start.15 = (s32[1,1,256]{2,1,0:T(1,128)S(1)}, s32[1,1,256]{2,1,0:T(1,128)}, u32[]{:S(2)}) copy-start(s32[1,1,256]{2,1,0:T(1,128)} %param.21) | copy-start | bytes 3076
  234.9 356.0 %all-to-all-start = ((f32[128,1,40]{2,1,0:T(1,128)}), f32[128,1,40]{2,1,0:T(1,128)}, u32[]{:S(2)}, u32[]{:S(2)}) async-start(f32[128,1,40]{2,1,0:T(1,128)} %bitcast.89), calls=%async_computation | async-start | bytes 131072 | tf_op jit(solution)/shard_map/all_to_all | solution.py:142
  249.9 6.1 copy-start.8
  251.1 4.5 collective-permute-start.1
  383.7 162.1 %copy-start.11 = (s32[8192,1]{0,1:T(1,128)S(1)}, s32[8192,1]{0,1:T(1,128)}, u32[]{:S(2)}) copy-start(s32[8192,1]{0,1:T(1,128)} %compare_select_fusion.1) | copy-start | bytes 98308
  542.4 4.1 collective-permute-start.2
  546.7 4.6 collective-permute-start.3
  551.4 31.0 %copy-start.12 = (f32[3,2048]{1,0:T(4,128)}, f32[3,2048]{1,0:T(4,128)S(1)}, u32[]{:S(2)}) copy-start(f32[3,2048]{1,0:T(4,128)S(1)} %fusion.37) | copy-start | bytes 73732
  551.7 30.7 %copy-start.5 = (f32[2048,128]{1,0:T(8,128)S(1)}, f32[2048,128]{1,0:T(8,128)}, u32[]{:S(2)}) copy-start(f32[2048,128]{1,0:T(8,128)} %fusion.40) | copy-start | bytes 3145732
  551.7 30.7 %copy-start.14 = (bf16[12,128]{1,0:T(8,128)(2,1)S(1)}, bf16[12,128]{1,0:T(8,128)(2,1)}, u32[]{:S(2)}) copy-start(bf16[12,128]{1,0:T(8,128)(2,1)} %param.28) | copy-start | bytes 9220
  590.8 54.2 %copy-start.1 = (bf16[384,128]{1,0:T(8,128)(2,1)S(1)}, bf16[384,128]{1,0:T(8,128)(2,1)}, u32[]{:S(2)}) copy-start(bf16[384,128]{1,0:T(8,128)(2,1)} %param.27) | copy-start | bytes 294916
  590.8 52.5 %all-to-all-start.1 = ((f32[128,40,128]{2,1,0:T(8,128)}), f32[128,40,128]{2,1,0:T(8,128)S(1)}, u32[]{:S(2)}, u32[]{:S(2)}) async-start(f32[128,40,128]{2,1,0:T(8,128)} %bitcast.22), calls=%async_computation.1 | async-start | bytes 5242880 | tf_op jit(solution)/shard_map/all_to_all | solution.py:135
where the time goes:
time: 646 us; the launch traced here: 645 us
  other arithmetic  340 us (53%)
  local copies, waits for them, and re-layouts  197 us (30%)
  waiting for transfers between devices  39.2 us (6%)
  starting transfers between devices  38.8 us (6%)
  matrix products  26.8 us (4%)
    scatter-add x2, other arithmetic, assemble(): jnp.zeros((fields, node_count), jnp.float32).at[:, conn_part.reshape(-1)]  333 us
    gather x4, local copies, waits for them, and re-layouts, at_elements(): return node_field[:, conn_part.reshape(-1)].reshape(fields * 4, -1)  149 us
    all_to_all x1, waiting for transfers between devices, per_device(): lax.all_to_all(payload.reshape(devices, capacity, block_width), ('dom', '...  32.9 us
    reshape x4, local copies, waits for them, and re-layouts, assemble(): flat_values = values.reshape(fields, -1)  18.3 us
    all_to_all x1, starting transfers between devices, per_device(): lax.all_to_all(payload.reshape(devices, capacity, block_width), ('dom', '...  17.3 us
  transfers between devices with their start and end apart: 6, of which 4 were waited for; matrix products, arithmetic and copies ran while one was open for 54% of the time, Pallas kernels for 0%

commit v1 on v0

v1 whole, which is shorter than its diff:
```python
import functools

import jax
import jax.numpy as jnp
from jax import lax
from jax.experimental import pallas as pl
from jax.experimental.pallas import tpu as pltpu
from jax.sharding import PartitionSpec as P

PATCH_DEV = 16
LANES = 128
HIS = 16
FIELDS = 3
RIM = 256

mass_shift = 0.5
relax = 0.7

f32 = jnp.float32
bf16 = jnp.bfloat16
VMEM_LIMIT = 60 * 2**20

NN = (((1,), (0,)), ((), ()))
NT = (((1,), (1,)), ((), ()))


def mxu(a, b, dims):
    return lax.dot_general(a, b, dims, preferred_element_type=f32)


def exact(a, b, dims):
    return lax.dot_general(
        a, b, dims, preferred_element_type=f32, precision=lax.Precision.HIGHEST
    )


def halves(x):
    top = x.astype(bf16).astype(f32)
    return top, x - top


def one_hot(index_row, rows):
    shape = (rows, index_row.shape[1])
    wanted = jnp.broadcast_to(index_row.astype(jnp.int16), shape)
    hit = wanted == lax.broadcasted_iota(jnp.int16, shape, 0)
    return jnp.where(hit, jnp.ones(shape, bf16), jnp.zeros(shape, bf16))


def placed(index_row, value_rows):
    shape = (HIS, index_row.shape[1])
    wanted = jnp.broadcast_to(index_row.astype(jnp.int16), shape)
    hit = wanted == lax.broadcasted_iota(jnp.int16, shape, 0)
    zero = jnp.zeros(shape, bf16)
    return jnp.concatenate(
        [jnp.where(hit, jnp.broadcast_to(v, shape).astype(bf16), zero) for v in value_rows], axis=0
    )


def rim_rows(field, first):
    count = field.shape[0] // HIS
    parts = [
        jnp.concatenate([field[f * HIS + first + k : f * HIS + first + k + 1] for f in range(count)], 0)
        for k in range(2)
    ]
    return jnp.concatenate(parts, axis=1)


def reorder(rows, perm_row, dims):
    count = rows.shape[0]
    table = one_hot(perm_row, RIM)
    first, rest = halves(rows)
    second, third = halves(rest)
    pad = jnp.zeros((-count % 8, RIM), f32)
    stack = jnp.concatenate([first, pad, second, pad, third, pad], axis=0).astype(bf16)
    out = mxu(stack, table, dims)
    step = count + (-count % 8)
    return out[:count] + out[step : step + count] + out[2 * step : 2 * step + count]


def add_rims(field, below, above, perm_row):
    count = field.shape[0] // HIS
    place = lax.axis_index("sub")
    last = lax.axis_size("sub") - 1
    below = jnp.where(place == 0, 0.0, below)
    above = jnp.where(place == last, 0.0, above)
    low = reorder(below, perm_row, NT)
    parts = []
    for f in range(count):
        rows = field[f * HIS : (f + 1) * HIS]
        extra = jnp.concatenate(
            [
                low[f : f + 1, :LANES],
                low[f : f + 1, LANES:],
                jnp.zeros((HIS - 4, LANES), f32),
                above[f : f + 1, :LANES],
                above[f : f + 1, LANES:],
            ],
            axis=0,
        )
        parts.append(rows + extra)
    return jnp.concatenate(parts, axis=0)


def front_kernel(
    traces, states, jac, stiff, conn, perm, ref, w_trace, w_state, w_node, w_block,
    field, up, low, blocks,
    trace_t, state_t, node_t, block_t, sens, weight,
):
    step = pl.program_id(0)

    @pl.when(step == 0)
    def _():
        trace_t[...] = w_trace[...].astype(f32).T.astype(bf16)
        state_t[...] = w_state[...].astype(f32).T.astype(bf16)
        padded = jnp.concatenate(
            [w_node[...].astype(f32).T, jnp.zeros((4, w_node.shape[0]), f32)], axis=0
        )
        node_t[...] = padded.astype(bf16)
        block_t[...] = w_block[...].astype(f32).T.astype(bf16)
        sens[...] = jnp.zeros(sens.shape, f32)
        weight[...] = jnp.zeros(weight.shape, f32)

    upsilon = mxu(trace_t[...], traces[...], NN)
    tangent = mxu(state_t[...], states[...], NN)
    product = (jac[...] * upsilon * tangent).astype(bf16)
    terms = mxu(node_t[...], product, NN)

    @pl.when(step == 0)
    def _():
        blocks[...] = mxu(block_t[...], product, NN)

    top, rest = halves(terms)
    stiff_top, stiff_rest = halves(stiff[...])
    slots = conn[...]
    high, lane = slots >> 7, slots & (LANES - 1)
    for a in range(4):
        rows = [top[c * 4 + a : c * 4 + a + 1] for c in range(FIELDS)] + [stiff_top]
        rows += [rest[c * 4 + a : c * 4 + a + 1] for c in range(FIELDS)] + [stiff_rest]
        spread = placed(high[a : a + 1], rows)
        out = mxu(spread, one_hot(lane[a : a + 1], LANES), NT)
        cut = FIELDS * HIS
        sens[...] += out[:cut] + out[cut + HIS : 2 * cut + HIS]
        weight[a * HIS : (a + 1) * HIS] += out[cut : cut + HIS] + out[2 * cut + HIS :]

    @pl.when(step == pl.num_programs(0) - 1)
    def _():
        diag = []
        for c in range(FIELDS):
            total = jnp.zeros((HIS, LANES), f32)
            for a in range(4):
                i = c * 4 + a
                total += ref[i : i + 1, i : i + 1] * weight[a * HIS : (a + 1) * HIS]
            diag.append(total)
        both = jnp.concatenate([sens[...]] + diag, axis=0)
        field[...] = both
        up[...] = rim_rows(both, HIS - 2)
        low[...] = reorder(rim_rows(both, 0), perm[...], NN)


def wall_kernel(blocks, owner, patch, sums):
    count = sums.shape[0]
    slot = patch[...] * (count // PATCH_DEV) + owner[...]
    table = one_hot(slot, count)
    top, rest = halves(blocks[...])
    both = jnp.concatenate([top, rest], axis=0).astype(bf16)
    out = mxu(table, both, NT)
    sums[...] = out[:, :LANES] + out[:, LANES:]


def looked_up(table, slots):
    count = table.shape[0] // HIS
    n = slots.shape[1] // LANES
    rows = [[] for _ in range(count)]
    for k in range(n):
        here = slots[:, k * LANES : (k + 1) * LANES]
        high, lane = here >> 7, here & (LANES - 1)
        for f in range(count):
            got = jnp.zeros((8, LANES), f32)
            for h in range(HIS):
                line = jnp.broadcast_to(table[f * HIS + h : f * HIS + h + 1], (8, LANES))
                picked = jnp.take_along_axis(line, lane, axis=1, mode="promise_in_bounds")
                got = jnp.where(high == h, picked, got)
            rows[f].append(got)
    return [jnp.concatenate(r, axis=1) for r in rows]


def apply_kernel(
    field, below, above, conn, stiff, perm, ref,
    base, scale, applied, up, low,
    *, chunk,
):
    shared = add_rims(field[...], below[...], above[...], perm[...])
    cut = FIELDS * HIS
    sens, diag = shared[:cut], shared[cut:] + mass_shift
    over = relax / diag
    psi = over * sens
    base[...] = psi + over * (sens - mass_shift * psi)
    scale[...] = over

    index = lax.broadcasted_iota(jnp.int32, (24, 12), 0)
    pick = (index // 8 * 4 + index % 4) == lax.broadcasted_iota(jnp.int32, (24, 12), 1)
    pick = pick.astype(f32)
    wide = exact(exact(pick, ref[...], NN), pick, NT)
    half_of_row = lax.broadcasted_iota(jnp.int32, (24, 24), 0) // 4 % 2
    half_of_col = lax.broadcasted_iota(jnp.int32, (24, 24), 1) // 4 % 2
    wide = jnp.where(half_of_row == half_of_col, wide, 0.0)
    wide_top, wide_rest = halves(wide)
    wide = jnp.concatenate(
        [
            jnp.concatenate([wide_top, wide_top], axis=1),
            jnp.concatenate([wide_rest, wide_rest], axis=1),
        ],
        axis=0,
    ).astype(bf16)

    half = conn.shape[1] // 2
    total = jnp.zeros((cut, LANES), f32)
    for start in range(0, half, chunk):
        first = slice(start, start + chunk)
        second = slice(half + start, half + start + chunk)
        slots = jnp.concatenate([conn[:, first], conn[:, second]], axis=0)
        values = jnp.concatenate(looked_up(psi, slots), axis=0)
        top, rest = halves(values)
        pushed = mxu(wide, jnp.concatenate([top, rest], axis=0).astype(bf16), NN)
        pushed = pushed[:24] + pushed[24:]
        in_first = lax.broadcasted_iota(jnp.int32, (8, chunk), 0) < 4
        weight = jnp.where(in_first, stiff[:, first], stiff[:, second])
        pushed = pushed * jnp.concatenate([weight] * FIELDS, axis=0)
        top, rest = halves(pushed)
        high, lane = slots >> 7, slots & (LANES - 1)
        for row in range(8):
            rows = [x[c * 8 + row : c * 8 + row + 1] for x in (top, rest) for c in range(FIELDS)]
            spread = placed(high[row : row + 1], rows)
            out = mxu(spread, one_hot(lane[row : row + 1], LANES), NT)
            total += out[:cut] + out[cut:]
    applied[...] = total
    up[...] = rim_rows(total, HIS - 2)
    low[...] = reorder(rim_rows(total, 0), perm[...], NN)


def patch_kernel(
    base, scale, applied, below, above, conn, owner, patch, perm, w_adjoint, sums,
    adjoint, payload,
):
    psi = base[...] - scale[...] * add_rims(applied[...], below[...], above[...], perm[...])
    for c in range(FIELDS):
        for h in range(HIS):
            adjoint[c : c + 1, h * LANES : (h + 1) * LANES] = psi[c * HIS + h : c * HIS + h + 1]
    half = conn.shape[1] // 2
    slots = jnp.concatenate([conn[:, :half], conn[:, half:]], axis=0)
    values = looked_up(psi, slots)
    parts = [halves(v) for v in values]
    owners = payload.shape[0] // PATCH_DEV
    total = jnp.zeros((owners, 24 * PATCH_DEV), f32)
    for k in range(2):
        cols = slice(k * half, (k + 1) * half)
        rows = [
            parts[c][p][4 * k + a : 4 * k + a + 1]
            for p in range(2)
            for c in range(FIELDS)
            for a in range(4)
        ]
        spread = placed(patch[:, cols], rows)
        total += mxu(one_hot(owner[:, cols], owners), spread, NT)
    total = total[:, : 12 * PATCH_DEV] + total[:, 12 * PATCH_DEV :]
    top, rest = halves(total)
    both = jnp.concatenate([top, rest], axis=0).astype(bf16)
    patch_row = lax.broadcasted_iota(jnp.int32, (PATCH_DEV, LANES), 0)
    weights = w_adjoint[...].astype(f32)
    for q in range(PATCH_DEV):
        chosen = jnp.concatenate(
            [jnp.where(patch_row == q, weights[r : r + 1], 0.0) for r in range(12)], axis=0
        ).astype(bf16)
        out = mxu(both, chosen, NN)
        payload[pl.ds(q, owners, stride=PATCH_DEV), :] = (
            out[:owners] + out[owners:] + sums[q * owners : (q + 1) * owners]
        )


def params(flops, bytes_accessed):
    return dict(
        compiler_params=pltpu.CompilerParams(vmem_limit_bytes=VMEM_LIMIT),
        cost_estimate=pl.CostEstimate(
            flops=flops, bytes_accessed=bytes_accessed, transcendentals=0
        ),
    )


def exchanged(up, low):
    count = lax.axis_size("sub")
    below = lax.ppermute(up, "sub", [(i, (i + 1) % count) for i in range(count)])
    above = lax.ppermute(low, "sub", [(i, (i - 1) % count) for i in range(count)])
    return below, above


def per_device(
    adjoint_traces,
    primal_traces,
    jacobian,
    stiffness,
    connect,
    shared_perm,
    wall_owner,
    wall_patch,
    w_trace,
    w_state,
    w_node,
    w_block,
    w_adjoint,
    stiff_ref,
):
    elements = adjoint_traces.shape[1]
    walls = wall_owner.shape[0]
    devices = lax.axis_size("dom") * lax.axis_size("sub")
    width = w_block.shape[1]
    jac = jacobian.reshape(1, -1)
    stiff = stiffness.reshape(1, -1)
    owner = wall_owner.reshape(1, -1)
    patch = wall_patch.reshape(1, -1)
    perm = shared_perm.reshape(1, -1)
    cut = FIELDS * HIS

    def whole(shape):
        return pl.BlockSpec(shape, lambda s: (0,) * len(shape))

    def columns(rows):
        return pl.BlockSpec((rows, walls), lambda s: (0, s))

    def shape(*dims):
        return jax.ShapeDtypeStruct(dims, f32)

    trace, quad = w_trace.shape
    outs = [shape(2 * cut, LANES), shape(6, RIM), shape(6, RIM), shape(width, walls)]
    field, up, low, blocks = pl.pallas_call(
        front_kernel,
        grid=(elements // walls,),
        in_specs=[
            columns(trace), columns(trace), columns(1), columns(1), columns(4),
            whole(perm.shape), whole(stiff_ref.shape), whole(w_trace.shape),
            whole(w_state.shape), whole(w_node.shape), whole(w_block.shape),
        ],
        out_specs=[whole(o.shape) for o in outs],
        out_shape=outs,
        scratch_shapes=[
            pltpu.VMEM((quad, trace), bf16),
            pltpu.VMEM((quad, trace), bf16),
            pltpu.VMEM((16, quad), bf16),
            pltpu.VMEM((width, quad), bf16),
            pltpu.VMEM((cut, LANES), f32),
            pltpu.VMEM((4 * HIS, LANES), f32),
        ],
        name="front",
        **params(4 * elements * trace * quad, 4 * elements * trace),
    )(
        adjoint_traces, primal_traces, jac, stiff, connect, perm, stiff_ref,
        w_trace, w_state, w_node, w_block,
    )
    below, above = exchanged(up, low)

    sums = pl.pallas_call(
        wall_kernel,
        out_shape=shape(devices * PATCH_DEV, width),
        name="walls",
        **params(4 * walls * width * devices * PATCH_DEV, 8 * walls * width),
    )(blocks, owner, patch)

    small = shape(cut, LANES)
    base, scale, applied, up, low = pl.pallas_call(
        functools.partial(apply_kernel, chunk=512),
        out_shape=[small, small, small, shape(3, RIM), shape(3, RIM)],
        name="apply",
        **params(16 * elements * LANES * cut, 24 * elements),
    )(field, below, above, connect, stiff, perm, stiff_ref)
    below, above = exchanged(up, low)

    adjoint, payload = pl.pallas_call(
        patch_kernel,
        grid=(1,),
        in_specs=[
            whole(small.shape), whole(small.shape), whole(small.shape),
            whole(below.shape), whole(above.shape),
            pl.BlockSpec((4, walls), lambda s: (0, 0)),
            whole(owner.shape), whole(patch.shape), whole(perm.shape),
            whole(w_adjoint.shape), whole(sums.shape),
        ],
        out_specs=[whole((FIELDS, HIS * LANES)), whole(sums.shape)],
        out_shape=[shape(FIELDS, HIS * LANES), shape(*sums.shape)],
        name="patches",
        **params(64 * walls * LANES * cut, 8 * devices * PATCH_DEV * width),
    )(base, scale, applied, below, above, connect, owner, patch, perm, w_adjoint, sums)

    got = lax.all_to_all(
        payload.reshape(devices, PATCH_DEV, width),
        ("dom", "sub"),
        split_axis=0,
        concat_axis=0,
        tiled=True,
    )
    return (jnp.sum(got, axis=0), adjoint)


def solution(mesh):
    both = ("dom", "sub")
    return jax.shard_map(
        per_device,
        mesh=mesh,
        in_specs=(
            P(None, both),
            P(None, both),
            P(both),
            P(both),
            P(None, both),
            P("dom", "sub", None),
            P(both, None),
            P(both),
            P(),
            P(),
            P(),
            P(),
            P(),
            P(),
        ),
        out_specs=(P(both, None), P(None, both)),
        check_vma=False,
    )
```

time: 646 us -> 71.9 us (0.11)
  other arithmetic: 340 us -> 0.73 us
  local copies, waits for them, and re-layouts: 197 us -> 2.65 us
  waiting for transfers between devices: 39.2 us -> 1.18 us
  Pallas kernels: 0 us -> 27.9 us
  starting transfers between devices: 38.8 us -> 11.7 us
  matrix products: 26.8 us -> 0 us
  blocking collectives: 0 us -> 26.7 us
    scatter-add x2 -> x0, other arithmetic: 333 us -> none  [assemble(): jnp.zeros((fields, node_count), jnp.float32).at[:, conn_part.reshape(-1)]]
    gather x5 -> x0, local copies, waits for them, and re-layouts: 149 us -> none  [the longest x4 149 us: at_elements(): return node_field[:, conn_part.reshape(-1)].reshape(fields * 4, -1)]
    all_to_all x2 -> x0, waiting for transfers between devices: 32.9 us -> none  [the longest x1 32.9 us: per_device(): lax.all_to_all(payload.reshape(devices, capacity, block_width), ('dom', '...]
    pallas_call x0 -> x4, Pallas kernels: none -> 27.9 us  [the longest x1 11.4 us: per_device(): pl.pallas_call(front_kernel, grid=(elements // walls,), in_specs=[columns...]
    all_to_all x2 -> x0, starting transfers between devices: 27.7 us -> none  [the longest x1 17.3 us: per_device(): lax.all_to_all(payload.reshape(devices, capacity, block_width), ('dom', '...]
    dot_general x17 -> x0, matrix products: 26.8 us -> none  [the longest x4 8.89 us: element_front(): upsilon = jnp.dot(w_trace.T, traces, preferred_element_type=jnp.float32)]
    all_to_all x0 -> x1, blocking collectives: none -> 26.7 us  [per_device(): lax.all_to_all(payload.reshape(devices, PATCH_DEV, width), ('dom', 'sub')...]
    reshape x6 -> x0, local copies, waits for them, and re-layouts: 18.6 us -> none  [the longest x4 18.3 us: assemble(): flat_values = values.reshape(fields, -1)]
  transfers between devices with their start and end apart: 6 -> 4, of which waited for: 4 -> 1; matrix products, arithmetic and copies ran while one was open for 54% -> 0% of each run, Pallas kernels for 0% -> 7%
where the time goes in v1:
time: 71.9 us; the launch traced here: 71.5 us
  Pallas kernels  27.9 us (39%)
  blocking collectives  26.7 us (37%)
  starting transfers between devices  11.7 us (16%)
  local copies, waits for them, and re-layouts  2.65 us (4%)
  waiting for transfers between devices  1.18 us (2%)
  other arithmetic  0.73 us (1%)
    all_to_all x1, blocking collectives, per_device(): lax.all_to_all(payload.reshape(devices, PATCH_DEV, width), ('dom', 'sub')...  26.7 us
    pallas_call x1, Pallas kernels, per_device(): pl.pallas_call(front_kernel, grid=(elements // walls,), in_specs=[columns...  11.4 us
    ppermute x2, starting transfers between devices, exchanged(): lax.ppermute(low, 'sub', [(i, (i - 1) % count) for i in range(count)])  9.24 us
    pallas_call x1, Pallas kernels, per_device(): pl.pallas_call(functools.partial(apply_kernel, chunk=512), out_shape=[sma...  7.16 us
    pallas_call x1, Pallas kernels, per_device(): pl.pallas_call(patch_kernel, grid=(1,), in_specs=[whole(small.shape), who...  4.7 us
    pallas_call x1, Pallas kernels, per_device(): pl.pallas_call(wall_kernel, out_shape=shape(devices * PATCH_DEV, width),...  4.65 us
    unnamed x9, local copies, waits for them, and re-layouts  2.65 us
    ppermute x2, starting transfers between devices, exchanged(): lax.ppermute(up, 'sub', [(i, (i + 1) % count) for i in range(count)])  2.47 us
  transfers between devices with their start and end apart: 4, of which 1 were waited for; matrix products, arithmetic and copies ran while one was open for 0% of the time, Pallas kernels for 7%

profile of v1, /device:TPU:1, one launch (start us, length us, event | category | flops | bytes accessed | tf_op | source)
XLA Modules:
  0.0 71.5 jit_solution(11135435021970738192)
XLA Ops:
  0.6 1.5 %copy.16.w_node = bf16[384,12]{1,0:T(8,128)(2,1)} copy(bf16[384,12]{0,1:T(8,128)(2,1)} %param.24) | data formatting | bytes 18432 | tf_op args[10]
  2.1 11.4 %front.1 = (f32[96,128]{1,0:T(8,128)}, f32[6,256]{1,0:T(8,128)}, f32[6,256]{1,0:T(8,128)}, f32[128,2048]{1,0:T(8,128)}) custom-call(bf16[144,8192]{1,0:T(8,128)(2,1)} %traces.1, bf16[144,8192]{1,0:T(8,128)(2,1)} %states.1, f32[1,8192]{1,0:T(1,128)} %bitcast.7, f32[1,8192]{1,0:T(1,128)} %bitcast.8, s32[4,8192]{1,0:T(4,128)} %conn.5, s32[1,256]{1,0:T(1,128)} %bitcast.14, ...), custom_call_target="tpu_custom_call" | custom-call | flops 1811939328 | bytes 4718592 | tf_op jit(solution)/shard_map/front/pallas_call | solution.py:334
  13.5 2.5 %collective-permute-start = (f32[6,256]{1,0:T(8,128)}, f32[6,256]{1,0:T(8,128)S(1)}, u32[]{:S(2)}, u32[]{:S(2)}) collective-permute-start(f32[6,256]{1,0:T(8,128)} %get-tuple-element.14), channel_id=1, source_target_pairs={{0,1},{1,2},{2,3},{3,4},{4,5},{5,6},{6,7},{7,8},{8,9},{9,10},{10,1... | collective-permute-start | bytes 18440 | tf_op jit(solution)/shard_map/ppermute | solution.py:291
  15.9 4.4 %collective-permute-start.1 = (f32[6,256]{1,0:T(8,128)}, f32[6,256]{1,0:T(8,128)S(1)}, u32[]{:S(2)}, u32[]{:S(2)}) collective-permute-start(f32[6,256]{1,0:T(8,128)} %get-tuple-element.15), channel_id=1, source_target_pairs={{0,15},{1,0},{2,1},{3,2},{4,3},{5,4},{6,5},{7,6},{8,7},{9,8},{10,9... | collective-permute-start | bytes 18440 | tf_op jit(solution)/shard_map/ppermute | solution.py:292
  20.3 1.2 %collective-permute-done.below = f32[6,256]{1,0:T(8,128)S(1)} collective-permute-done((f32[6,256]{1,0:T(8,128)}, f32[6,256]{1,0:T(8,128)S(1)}, u32[]{:S(2)}, u32[]{:S(2)}) %collective-permute-start) | collective-permute-done | bytes 6176 | tf_op jit(solution)/shard_map/ppermute | solution.py:291
  21.5 0.0 copy-start
  21.5 0.0 collective-permute-done.1.above
  21.5 0.0 copy-start.1
  21.5 0.6 copy-done
  22.1 0.0 copy-done.1
  22.1 7.2 %apply.1 = (f32[48,128]{1,0:T(8,128)}, f32[48,128]{1,0:T(8,128)}, f32[48,128]{1,0:T(8,128)}, f32[3,256]{1,0:T(4,128)}, f32[3,256]{1,0:T(4,128)}) custom-call(f32[96,128]{1,0:T(8,128)} %get-tuple-element.13.field, f32[6,256]{1,0:T(8,128)} %copy-done, f32[6,256]{1,0:T(8,128)} %copy-done.1, s32[4,8192]{1,0:T(4,128)} %conn.5, f32[1,8192]{1,0:T(1,128)} %bitcast.9, ...), custom_call_target="tpu_custom_call" | custom-call | flops 805306368 | bytes 196608 | tf_op jit(solution)/shard_map/apply/pallas_call | solution.py:368
  29.3 0.0 collective-permute-start.2
  29.3 4.9 %collective-permute-start.3 = (f32[3,256]{1,0:T(4,128)}, f32[3,256]{1,0:T(4,128)S(1)}, u32[]{:S(2)}, u32[]{:S(2)}) collective-permute-start(f32[3,256]{1,0:T(4,128)} %get-tuple-element.20), channel_id=1, source_target_pairs={{0,15},{1,0},{2,1},{3,2},{4,3},{5,4},{6,5},{7,6},{8,7},{9,8},{10,9... | collective-permute-start | bytes 9224 | tf_op jit(solution)/shard_map/ppermute | solution.py:292
  34.1 4.7 %walls.1.sums = f32[2048,128]{1,0:T(8,128)} custom-call(f32[128,2048]{1,0:T(8,128)} %get-tuple-element.21.blocks, s32[1,2048]{1,0:T(1,128)} %bitcast.10, s32[1,2048]{1,0:T(1,128)} %bitcast.12), custom_call_target="tpu_custom_call" | custom-call | flops 2147483648 | bytes 2097152 | tf_op jit(solution)/shard_map/walls/pallas_call | solution.py:360
  38.8 0.0 collective-permute-done.2.below
  38.8 0.0 copy-start.2
  38.8 0.0 collective-permute-done.3.above
  38.8 0.0 copy-start.3
  38.8 0.6 copy-done.2
  39.4 0.0 copy-done.3
  39.4 4.7 %patches.1 = (f32[3,2048]{1,0:T(4,128)}, f32[2048,128]{1,0:T(8,128)}) custom-call(f32[48,128]{1,0:T(8,128)} %get-tuple-element.16.base, f32[48,128]{1,0:T(8,128)} %get-tuple-element.17.scale, f32[48,128]{1,0:T(8,128)} %get-tuple-element.18.applied, f32[3,256]{1,0:T(4,128)} %copy-done.2, f32[3,256]{1,0:T(4,128)} %copy-done.3, s32[4,8192]{1,0:T(4,128)} %conn.5, ...), custom_call_target="tpu_custom_call" | custom-call | flops 805306368 | bytes 2097152 | tf_op jit(solution)/shard_map/patches/pallas_call | solution.py:376
  44.1 26.7 %all_to_all.5 = f32[128,16,128]{2,1,0:T(8,128)S(1)} all-to-all(f32[128,16,128]{2,1,0:T(8,128)} %bitcast.6), channel_id=1, replica_groups=mesh['dom'=8,'sub'=16] {'dom','sub'}, dimensions={0} | all-to-all | bytes 2097152 | tf_op jit(solution)/shard_map/all_to_all | solution.py:392
  70.8 0.7 %reduce_sum.9 = f32[16,128]{1,0:T(8,128)} reduce(f32[128,16,128]{2,1,0:T(8,128)S(1)} %all_to_all.5, f32[]{:T(128)} %constant.0.clone.1), dimensions={0}, to_apply=%region_0.0 | reduce | flops 260096 | bytes 1056772 | tf_op jit(solution)/shard_map/reduce_sum | solution.py:399
Async XLA Ops:
  13.5 8.0 %collective-permute-start = (f32[6,256]{1,0:T(8,128)}, f32[6,256]{1,0:T(8,128)S(1)}, u32[]{:S(2)}, u32[]{:S(2)}) collective-permute-start(f32[6,256]{1,0:T(8,128)} %get-tuple-element.14), channel_id=1, source_target_pairs={{0,1},{1,2},{2,3},{3,4},{4,5},{5,6},{6,7},{7,8},{8,9},{9,10},{10,1... | collective-permute-start | bytes 18440 | tf_op jit(solution)/shard_map/ppermute | solution.py:291
  15.9 5.6 %collective-permute-start.1 = (f32[6,256]{1,0:T(8,128)}, f32[6,256]{1,0:T(8,128)S(1)}, u32[]{:S(2)}, u32[]{:S(2)}) collective-permute-start(f32[6,256]{1,0:T(8,128)} %get-tuple-element.15), channel_id=1, source_target_pairs={{0,15},{1,0},{2,1},{3,2},{4,3},{5,4},{6,5},{7,6},{8,7},{9,8},{10,9... | collective-permute-start | bytes 18440 | tf_op jit(solution)/shard_map/ppermute | solution.py:292
  21.5 0.6 copy-start
  21.5 0.6 copy-start.1
  29.3 9.5 %collective-permute-start.2 = (f32[3,256]{1,0:T(4,128)}, f32[3,256]{1,0:T(4,128)S(1)}, u32[]{:S(2)}, u32[]{:S(2)}) collective-permute-start(f32[3,256]{1,0:T(4,128)} %get-tuple-element.19), channel_id=1, source_target_pairs={{0,1},{1,2},{2,3},{3,4},{4,5},{5,6},{6,7},{7,8},{8,9},{9,10},{10,1... | collective-permute-start | bytes 9224 | tf_op jit(solution)/shard_map/ppermute | solution.py:291
  29.3 9.5 %collective-permute-start.3 = (f32[3,256]{1,0:T(4,128)}, f32[3,256]{1,0:T(4,128)S(1)}, u32[]{:S(2)}, u32[]{:S(2)}) collective-permute-start(f32[3,256]{1,0:T(4,128)} %get-tuple-element.20), channel_id=1, source_target_pairs={{0,15},{1,0},{2,1},{3,2},{4,3},{5,4},{6,5},{7,6},{8,7},{9,8},{10,9... | collective-permute-start | bytes 9224 | tf_op jit(solution)/shard_map/ppermute | solution.py:292
  38.8 0.6 copy-start.2
  38.8 0.6 copy-start.3

commit v2 on v1

v2 whole, which is shorter than its diff:
```python
import functools

import jax
import jax.numpy as jnp
from jax import lax
from jax.experimental import pallas as pl
from jax.experimental.pallas import tpu as pltpu
from jax.sharding import PartitionSpec as P

PATCH_DEV = 16
LANES = 128
HIS = 16
FIELDS = 3
RIM = 256
GROUP = 4
KEPT = PATCH_DEV // GROUP
FRONT_VMEM = 40
ROWS = 8

mass_shift = 0.5
relax = 0.7

f32 = jnp.float32
bf16 = jnp.bfloat16

NN = (((1,), (0,)), ((), ()))
NT = (((1,), (1,)), ((), ()))


def mxu(a, b, dims):
    return lax.dot_general(a, b, dims, preferred_element_type=f32)


def exact(a, b, dims):
    return lax.dot_general(
        a, b, dims, preferred_element_type=f32, precision=lax.Precision.HIGHEST
    )


def halves(x):
    top = x.astype(bf16).astype(f32)
    return top, x - top


def one_hot(index_row, rows):
    shape = (rows, index_row.shape[1])
    wanted = jnp.broadcast_to(index_row.astype(jnp.int16), shape)
    hit = wanted == lax.broadcasted_iota(jnp.int16, shape, 0)
    return jnp.where(hit, jnp.ones(shape, bf16), jnp.zeros(shape, bf16))


def placed(index_row, value_rows):
    shape = (HIS, index_row.shape[1])
    wanted = jnp.broadcast_to(index_row.astype(jnp.int16), shape)
    hit = wanted == lax.broadcasted_iota(jnp.int16, shape, 0)
    zero = jnp.zeros(shape, bf16)
    return jnp.concatenate(
        [jnp.where(hit, jnp.broadcast_to(v, shape).astype(bf16), zero) for v in value_rows], axis=0
    )


def rim_rows(field, first):
    count = field.shape[0] // HIS
    parts = [
        jnp.concatenate([field[f * HIS + first + k : f * HIS + first + k + 1] for f in range(count)], 0)
        for k in range(2)
    ]
    return jnp.concatenate(parts, axis=1)


def reorder(rows, perm_row, dims):
    count = rows.shape[0]
    table = one_hot(perm_row, RIM)
    first, rest = halves(rows)
    second, third = halves(rest)
    pad = jnp.zeros((-count % 8, RIM), f32)
    stack = jnp.concatenate([first, pad, second, pad, third, pad], axis=0).astype(bf16)
    out = mxu(stack, table, dims)
    step = count + (-count % 8)
    return out[:count] + out[step : step + count] + out[2 * step : 2 * step + count]


def rims(below, above, perm_row):
    count = below.shape[0]
    place = lax.axis_index("sub")
    last = lax.axis_size("sub") - 1
    below = jnp.where(place == 0, 0.0, below)
    above = jnp.where(place == last, 0.0, above)
    low = reorder(below, perm_row, NT)
    parts = []
    for f in range(count):
        parts += [
            low[f : f + 1, :LANES],
            low[f : f + 1, LANES:],
            jnp.zeros((HIS - 4, LANES), f32),
            above[f : f + 1, :LANES],
            above[f : f + 1, LANES:],
        ]
    return jnp.concatenate(parts, axis=0)


def front_kernel(*refs, walls):
    sources, (field, up, low, blocks), held, sems = refs[:11], refs[11:15], refs[15:26], refs[26]
    traces, states, jac, stiff, conn, w_trace, w_state, w_node, w_block, perm, ref = held
    spans = [slice(s, s + walls) for s in range(0, traces.shape[1], walls)]
    copies = []

    def fetch(k, span=None):
        source, target = sources[k], held[k]
        if span is not None:
            source, target = source.at[:, span], target.at[:, span]
        copy = pltpu.make_async_copy(source, target, sems.at[len(copies)])
        copy.start()
        copies.append(copy)
        return copy

    weights = [fetch(k) for k in (5, 6, 7, 8)]
    first = [fetch(0, spans[0]), fetch(1, spans[0]), fetch(2)]
    small = [fetch(k) for k in (3, 4)]
    later = [[fetch(0, span), fetch(1, span)] for span in spans[1:]]
    last = [fetch(k) for k in (9, 10)]
    for copy in weights:
        copy.wait()
    trace_t = w_trace[...].astype(f32).T.astype(bf16)
    state_t = w_state[...].astype(f32).T.astype(bf16)
    pad = jnp.zeros((4, w_node.shape[1]), f32)
    node_t = jnp.concatenate([w_node[...].astype(f32), pad], axis=0).astype(bf16)
    block_t = w_block[...].astype(f32).T.astype(bf16)
    cut = FIELDS * HIS
    sens = jnp.zeros((cut, LANES), f32)
    weight = [jnp.zeros((HIS, LANES), f32) for _ in range(4)]
    for s, span in enumerate(spans):
        for copy in first if s == 0 else later[s - 1]:
            copy.wait()
        upsilon = mxu(trace_t, traces[:, span], NN)
        tangent = mxu(state_t, states[:, span], NN)
        product = (jac[:, span] * upsilon * tangent).astype(bf16)
        terms = mxu(node_t, product, NN)
        if s == 0:
            blocks[...] = mxu(block_t, product, NN)
            for copy in small:
                copy.wait()
        top, rest = halves(terms)
        stiff_top, stiff_rest = halves(stiff[:, span])
        slots = conn[:, span]
        high, lane = slots >> 7, slots & (LANES - 1)
        for a in range(4):
            rows = [top[c * 4 + a : c * 4 + a + 1] for c in range(FIELDS)] + [stiff_top]
            rows += [rest[c * 4 + a : c * 4 + a + 1] for c in range(FIELDS)] + [stiff_rest]
            spread = placed(high[a : a + 1], rows)
            out = mxu(spread, one_hot(lane[a : a + 1], LANES), NT)
            sens += out[:cut] + out[cut + HIS : 2 * cut + HIS]
            weight[a] += out[cut : cut + HIS] + out[2 * cut + HIS :]

    for copy in last:
        copy.wait()
    diag = []
    for c in range(FIELDS):
        total = jnp.zeros((HIS, LANES), f32)
        for a in range(4):
            i = c * 4 + a
            total += ref[i : i + 1, i : i + 1] * weight[a]
        diag.append(total)
    both = jnp.concatenate([sens] + diag, axis=0)
    field[...] = both
    up[...] = rim_rows(both, HIS - 2)
    low[...] = reorder(rim_rows(both, 0), perm[...], NN)


def group_place():
    return lax.axis_index("dom") % GROUP


def wall_kernel(blocks, owner, patch, *sums):
    rows = sums[0].shape[0]
    slot = (patch[...] // KEPT ^ group_place()) * rows + owner[...] * KEPT + patch[...] % KEPT
    top, rest = halves(blocks[...])
    both = jnp.concatenate([top, rest], axis=0).astype(bf16)
    for k in range(GROUP):
        out = mxu(one_hot(slot - k * rows, rows), both, NT)
        sums[k][...] = out[:, :LANES] + out[:, LANES:]


def looked_up(table, slots, lines):
    count = table.shape[0] // HIS
    n = slots.shape[1] // LANES
    rows = [[] for _ in range(count)]
    for k in range(n):
        here = slots[:, k * LANES : (k + 1) * LANES]
        high, lane = here >> 7, here & (LANES - 1)
        for f in range(count):
            got = jnp.zeros((8, LANES), f32)
            for h in lines:
                line = jnp.broadcast_to(table[f * HIS + h : f * HIS + h + 1], (8, LANES))
                picked = jnp.take_along_axis(line, lane, axis=1, mode="promise_in_bounds")
                got = jnp.where(high == h, picked, got)
            rows[f].append(got)
    return [jnp.concatenate(r, axis=1) for r in rows]


def apply_kernel(
    field, below, above, conn, stiff, perm, ref,
    base, scale, applied, up, low,
    *, chunk,
):
    shared = field[...] + rims(below[...], above[...], perm[...])
    cut = FIELDS * HIS
    sens, diag = shared[:cut], shared[cut:] + mass_shift
    over = relax / diag
    psi = over * sens
    base[...] = psi + over * (sens - mass_shift * psi)
    scale[...] = over

    index = lax.broadcasted_iota(jnp.int32, (24, 12), 0)
    pick = (index // 8 * 4 + index % 4) == lax.broadcasted_iota(jnp.int32, (24, 12), 1)
    pick = pick.astype(f32)
    wide = exact(exact(pick, ref[...], NN), pick, NT)
    half_of_row = lax.broadcasted_iota(jnp.int32, (24, 24), 0) // 4 % 2
    half_of_col = lax.broadcasted_iota(jnp.int32, (24, 24), 1) // 4 % 2
    wide = jnp.where(half_of_row == half_of_col, wide, 0.0)
    wide_top, wide_rest = halves(wide)
    wide = jnp.concatenate(
        [
            jnp.concatenate([wide_top, wide_top], axis=1),
            jnp.concatenate([wide_rest, wide_rest], axis=1),
        ],
        axis=0,
    ).astype(bf16)

    half = conn.shape[1] // 2
    total = jnp.zeros((cut, LANES), f32)
    for start in range(0, half, chunk):
        first = slice(start, start + chunk)
        second = slice(half + start, half + start + chunk)
        slots = jnp.concatenate([conn[:, first], conn[:, second]], axis=0)
        values = jnp.concatenate(looked_up(psi, slots, range(HIS)), axis=0)
        top, rest = halves(values)
        pushed = mxu(wide, jnp.concatenate([top, rest], axis=0).astype(bf16), NN)
        pushed = pushed[:24] + pushed[24:]
        in_first = lax.broadcasted_iota(jnp.int32, (8, chunk), 0) < 4
        weight = jnp.where(in_first, stiff[:, first], stiff[:, second])
        pushed = pushed * jnp.concatenate([weight] * FIELDS, axis=0)
        top, rest = halves(pushed)
        high, lane = slots >> 7, slots & (LANES - 1)
        for row in range(8):
            rows = [x[c * 8 + row : c * 8 + row + 1] for x in (top, rest) for c in range(FIELDS)]
            spread = placed(high[row : row + 1], rows)
            out = mxu(spread, one_hot(lane[row : row + 1], LANES), NT)
            total += out[:cut] + out[cut:]
    applied[...] = total
    up[...] = rim_rows(total, HIS - 2)
    low[...] = reorder(rim_rows(total, 0), perm[...], NN)


def patch_sums(values, owner, patch, owners):
    half = values[0].shape[1]
    parts = [halves(v) for v in values]
    total = jnp.zeros((owners, 24 * PATCH_DEV), f32)
    for k in range(2):
        cols = slice(k * half, (k + 1) * half)
        rows = [
            parts[c][p][4 * k + a : 4 * k + a + 1]
            for p in range(2)
            for c in range(FIELDS)
            for a in range(4)
        ]
        spread = placed(patch[:, cols], rows)
        total += mxu(one_hot(owner[:, cols], owners), spread, NT)
    return total[:, : 12 * PATCH_DEV] + total[:, 12 * PATCH_DEV :]


def wall_slots(conn):
    half = conn.shape[1] // 2
    return jnp.concatenate([conn[:, :half], conn[:, half:]], axis=0)


def local_kernel(base, scale, applied, conn, owner, patch, local, sums):
    psi = base[...] - scale[...] * applied[...]
    local[...] = psi
    values = looked_up(psi, wall_slots(conn), range(HIS))
    sums[:, : 12 * PATCH_DEV] = patch_sums(values, owner, patch, sums.shape[0])
    sums[:, 12 * PATCH_DEV :] = jnp.zeros((sums.shape[0], 4 * PATCH_DEV), f32)


def rim_kernel(
    local, scale, below, above, conn, owner, patch, perm, sums, *rest
):
    *pieces, adjoint, payload = rest
    change = -scale[...] * rims(below[...], above[...], perm[...])
    psi = local[...] + change
    for c in range(FIELDS):
        for h in range(HIS):
            adjoint[c : c + 1, h * LANES : (h + 1) * LANES] = psi[c * HIS + h : c * HIS + h + 1]
    values = looked_up(change, wall_slots(conn), (0, 1, HIS - 2, HIS - 1))
    owners = sums.shape[0]
    more = patch_sums(values, owner, patch, owners)
    total = sums[...] + jnp.concatenate([more, jnp.zeros((owners, 4 * PATCH_DEV), f32)], axis=1)
    kept = pieces[0][...]
    for piece in pieces[1:]:
        kept += piece[...]
    payload[:, :KEPT, :] = kept.reshape(owners, KEPT, LANES)
    payload[:, KEPT : KEPT + 1, :] = total[:, :LANES].reshape(owners, 1, LANES)
    payload[:, KEPT + 1 : KEPT + 2, :] = total[:, LANES:].reshape(owners, 1, LANES)
    payload[:, KEPT + 2 :, :] = jnp.zeros((owners, ROWS - KEPT - 2, LANES), f32)


def owner_kernel(got, w_adjoint, out):
    doms = lax.axis_size("dom")
    subs = got.shape[0] // doms
    by_dom = []
    for d in range(doms):
        total = got[d * subs]
        for s in range(1, subs):
            total += got[d * subs + s]
        by_dom.append(total)
    parts = []
    for g in range(GROUP):
        total = by_dom[g]
        for d in range(g + GROUP, doms, GROUP):
            total += by_dom[d]
        parts.append(total[:KEPT])
    everything = by_dom[0]
    for d in range(1, doms):
        everything += by_dom[d]
    shape = (PATCH_DEV, LANES)
    mine = lax.broadcasted_iota(jnp.int32, shape, 1) % PATCH_DEV == lax.broadcasted_iota(
        jnp.int32, shape, 0
    )
    spread = [
        jnp.where(mine, everything[KEPT + k : KEPT + k + 1], 0.0) for k in range(2)
    ]
    shape = (2 * LANES, w_adjoint.shape[0])
    rows = lax.broadcasted_iota(jnp.int32, shape, 0) // PATCH_DEV
    pick = (rows == lax.broadcasted_iota(jnp.int32, shape, 1)).astype(f32)
    weights = exact(pick, w_adjoint[...].astype(f32), NN)
    out[...] = jnp.concatenate(parts, axis=0) + exact(
        jnp.concatenate(spread, axis=1), weights, NN
    )


def params(flops, bytes_accessed, vmem=24):
    return dict(
        compiler_params=pltpu.CompilerParams(vmem_limit_bytes=vmem * 2**20),
        cost_estimate=pl.CostEstimate(
            flops=flops, bytes_accessed=bytes_accessed, transcendentals=0
        ),
    )


def whole(shape):
    return pl.BlockSpec(shape, lambda s: (0,) * len(shape))


def shape(*dims):
    return jax.ShapeDtypeStruct(dims, f32)


def front(walls, *fetched):
    trace, elements = fetched[0].shape
    quad, width = fetched[8].shape
    outs = [shape(2 * FIELDS * HIS, LANES), shape(6, RIM), shape(6, RIM), shape(width, walls)]
    copies = len(fetched) + 2 * (elements // walls - 1)
    return pl.pallas_call(
        functools.partial(front_kernel, walls=walls),
        in_specs=[pl.BlockSpec(memory_space=pl.ANY)] * len(fetched),
        out_shape=outs,
        scratch_shapes=[
            *(pltpu.VMEM(x.shape, x.dtype) for x in fetched),
            pltpu.SemaphoreType.DMA((copies,)),
        ],
        name="front",
        **params(4 * elements * trace * quad, 4 * elements * trace, FRONT_VMEM),
    )(*(pltpu.with_memory_space_constraint(x, pltpu.HBM) for x in fetched))


def apply(field, below, above, connect, stiff, perm, stiff_ref):
    elements = connect.shape[1]
    cut = FIELDS * HIS
    small = shape(cut, LANES)
    return pl.pallas_call(
        functools.partial(apply_kernel, chunk=512),
        out_shape=[small, small, small, shape(3, RIM), shape(3, RIM)],
        name="apply",
        **params(16 * elements * LANES * cut, 24 * elements),
    )(field, below, above, connect, stiff, perm, stiff_ref)


def exchanged(up, low):
    count = lax.axis_size("sub")
    below = lax.ppermute(up, "sub", [(i, (i + 1) % count) for i in range(count)])
    above = lax.ppermute(low, "sub", [(i, (i - 1) % count) for i in range(count)])
    return below, above


def per_device(
    adjoint_traces,
    primal_traces,
    jacobian,
    stiffness,
    connect,
    shared_perm,
    wall_owner,
    wall_patch,
    w_trace,
    w_state,
    w_node,
    w_block,
    w_adjoint,
    stiff_ref,
):
    walls = wall_owner.shape[0]
    devices = lax.axis_size("dom") * lax.axis_size("sub")
    width = w_block.shape[1]
    jac = jacobian.reshape(1, -1)
    stiff = stiffness.reshape(1, -1)
    owner = wall_owner.reshape(1, -1)
    patch = wall_patch.reshape(1, -1)
    perm = shared_perm.reshape(1, -1)
    field, up, low, blocks = front(
        walls, adjoint_traces, primal_traces, jac, stiff, connect,
        w_trace, w_state, w_node.T, w_block, perm, stiff_ref,
    )
    below, above = exchanged(up, low)

    pieces = pl.pallas_call(
        wall_kernel,
        out_shape=[shape(devices * KEPT, width)] * GROUP,
        name="walls",
        **params(4 * walls * width * devices * PATCH_DEV, 8 * walls * width),
    )(blocks, owner, patch)
    *pieces, below, above = lax.optimization_barrier((*pieces, below, above))
    doms = lax.axis_size("dom")
    pieces = [
        pieces[0],
        *(
            lax.ppermute(pieces[k], "dom", [(i, i ^ k) for i in range(doms)])
            for k in range(1, GROUP)
        ),
    ]

    small = shape(FIELDS * HIS, LANES)
    base, scale, applied, up, low = apply(
        field, below, above, connect, stiff, perm, stiff_ref
    )
    below, above = exchanged(up, low)

    conn_spec = pl.BlockSpec((4, walls), lambda s: (0, 0))
    local, sums = pl.pallas_call(
        local_kernel,
        grid=(1,),
        in_specs=[
            *[whole(small.shape)] * 3, conn_spec, whole(owner.shape), whole(patch.shape),
        ],
        out_specs=[whole(small.shape), whole((devices, 2 * LANES))],
        out_shape=[small, shape(devices, 2 * LANES)],
        name="local",
        **params(3000 * walls * LANES, 8 * devices * PATCH_DEV * width),
    )(base, scale, applied, connect, owner, patch)

    adjoint, payload = pl.pallas_call(
        rim_kernel,
        grid=(1,),
        in_specs=[
            *[whole(small.shape)] * 2, whole(below.shape), whole(above.shape), conn_spec,
            whole(owner.shape), whole(patch.shape), whole(perm.shape), whole(sums.shape),
            *[whole(pieces[0].shape)] * GROUP,
        ],
        out_specs=[whole((FIELDS, HIS * LANES)), whole((devices, ROWS, LANES))],
        out_shape=[shape(FIELDS, HIS * LANES), shape(devices, ROWS, LANES)],
        name="rims",
        **params(3000 * walls * LANES, 8 * devices * PATCH_DEV * width),
    )(local, scale, below, above, connect, owner, patch, perm, sums, *pieces)

    got = lax.all_to_all(payload, ("dom", "sub"), split_axis=0, concat_axis=0, tiled=True)
    grad = pl.pallas_call(
        owner_kernel,
        out_shape=shape(PATCH_DEV, width),
        name="owners",
        **params(10**6, 4 * devices * ROWS * width),
    )(got, w_adjoint)
    return (grad, adjoint)


def solution(mesh):
    both = ("dom", "sub")
    return jax.shard_map(
        per_device,
        mesh=mesh,
        in_specs=(
            P(None, both),
            P(None, both),
            P(both),
            P(both),
            P(None, both),
            P("dom", "sub", None),
            P(both, None),
            P(both),
            P(),
            P(),
            P(),
            P(),
            P(),
            P(),
        ),
        out_specs=(P(both, None), P(None, both)),
        check_vma=False,
    )
```

time: 71.9 us -> 62.9 us (0.87)
  blocking collectives: 26.7 us -> 22.6 us
  Pallas kernels: 27.9 us -> 24.6 us
  starting transfers between devices: 11.7 us -> 14.5 us
  local copies, waits for them, and re-layouts: 2.65 us -> 0.03 us
  waiting for transfers between devices: 1.18 us -> 0.31 us
  other arithmetic: 0.73 us -> 0 us
    all_to_all x1, blocking collectives: 26.7 us -> 22.6 us  [per_device(): lax.all_to_all(payload, ('dom', 'sub'), split_axis=0, concat_axis=0, tile...]
    pallas_call x4 -> x6, Pallas kernels: 27.9 us -> 24.6 us  [the longest x1 12.9 us: front(): pl.pallas_call(functools.partial(front_kernel, walls=walls), in_specs=[pl...]
    ppermute x0 -> x3, starting transfers between devices: none -> 2.76 us  [per_device(): lax.ppermute(pieces[k], 'dom', [(i, i ^ k) for i in range(doms)])]
    unnamed x9 -> x14, local copies, waits for them, and re-layouts: 2.65 us -> 0.03 us
    ppermute x2, waiting for transfers between devices: 1.17 us -> 0.01 us  [exchanged(): lax.ppermute(up, 'sub', [(i, (i + 1) % count) for i in range(count)])]
    reduce_sum x1 -> x0, other arithmetic: 0.73 us -> none  [per_device(): return (jnp.sum(got, axis=0), adjoint)]
  transfers between devices with their start and end apart: 4 -> 7, of which waited for: 1 -> 1; matrix products, arithmetic and copies ran while one was open for 0% -> 0% of each run, Pallas kernels for 7% -> 15%
where the time goes in v2:
time: 62.9 us; the launch traced here: 62.8 us
  Pallas kernels  24.6 us (39%)
  blocking collectives  22.6 us (36%)
  starting transfers between devices  14.5 us (23%)
  between operations  0.77 us (1%)
    all_to_all x1, blocking collectives, per_device(): lax.all_to_all(payload, ('dom', 'sub'), split_axis=0, concat_axis=0, tile...  22.6 us
    pallas_call x1, Pallas kernels, front(): pl.pallas_call(functools.partial(front_kernel, walls=walls), in_specs=[pl...  12.9 us
    ppermute x2, starting transfers between devices, exchanged(): lax.ppermute(low, 'sub', [(i, (i - 1) % count) for i in range(count)])  9.19 us
    pallas_call x1, Pallas kernels, apply(): pl.pallas_call(functools.partial(apply_kernel, chunk=512), out_shape=[sma...  5.64 us
    ppermute x3, starting transfers between devices, per_device(): lax.ppermute(pieces[k], 'dom', [(i, i ^ k) for i in range(doms)])  2.76 us
    ppermute x2, starting transfers between devices, exchanged(): lax.ppermute(up, 'sub', [(i, (i + 1) % count) for i in range(count)])  2.54 us
    pallas_call x1, Pallas kernels, per_device(): pl.pallas_call(wall_kernel, out_shape=[shape(devices * KEPT, width)] * GR...  2.36 us
    pallas_call x1, Pallas kernels, per_device(): pl.pallas_call(local_kernel, grid=(1,), in_specs=[*[whole(small.shape)] *...  1.43 us
  transfers between devices with their start and end apart: 7, of which 1 were waited for; matrix products, arithmetic and copies ran while one was open for 0% of the time, Pallas kernels for 15%

profile of v2, /device:TPU:1, one launch (start us, length us, event | category | flops | bytes accessed | tf_op | source)
XLA Modules:
  0.0 62.8 jit_solution(14455075008058119986)
XLA Ops:
  0.6 0.0 copy-start.4
  0.6 0.0 copy-start.5
  0.7 12.9 %front.1 = (f32[96,128]{1,0:T(8,128)S(1)}, f32[6,256]{1,0:T(8,128)S(1)}, f32[6,256]{1,0:T(8,128)S(1)}, f32[128,2048]{1,0:T(8,128)S(1)}) custom-call(bf16[144,8192]{1,0:T(8,128)(2,1)} %refs_0_.1, bf16[144,8192]{1,0:T(8,128)(2,1)} %refs_1_.1, f32[1,8192]{1,0:T(1,128)} %bitcast.17, f32[1,8192]{1,0:T(1,128)} %bitcast.6, s32[4,8192]{1,0:T(4,128)} %conn.5, ...), custom_call_target="tpu_custom_call" | custom-call | flops 1811939328 | bytes 4718592 | tf_op jit(solution)/shard_map/front/pallas_call | solution.py:363
  13.6 2.5 %collective-permute-start = (f32[6,256]{1,0:T(8,128)S(1)}, f32[6,256]{1,0:T(8,128)S(1)}, u32[]{:S(2)}, u32[]{:S(2)}) collective-permute-start(f32[6,256]{1,0:T(8,128)S(1)} %get-tuple-element.31), channel_id=1, source_target_pairs={{0,1},{1,2},{2,3},{3,4},{4,5},{5,6},{6,7},{7,8},{8,9},{9,10},{10,1... | collective-permute-start | bytes 18440 | tf_op jit(solution)/shard_map/ppermute | solution.py:390
  16.1 4.4 %collective-permute-start.1 = (f32[6,256]{1,0:T(8,128)S(1)}, f32[6,256]{1,0:T(8,128)S(1)}, u32[]{:S(2)}, u32[]{:S(2)}) collective-permute-start(f32[6,256]{1,0:T(8,128)S(1)} %get-tuple-element.32), channel_id=1, source_target_pairs={{0,15},{1,0},{2,1},{3,2},{4,3},{5,4},{6,5},{7,6},{8,7},{9,8},{10,9... | collective-permute-start | bytes 18440 | tf_op jit(solution)/shard_map/ppermute | solution.py:391
  20.5 0.0 copy-done.4
  20.5 0.0 copy-done.5
  20.5 0.0 copy-start.3
  20.6 0.0 copy-start.6
  20.6 2.4 %walls.1 = (f32[512,128]{1,0:T(8,128)S(1)}, f32[512,128]{1,0:T(8,128)S(1)}, f32[512,128]{1,0:T(8,128)S(1)}, f32[512,128]{1,0:T(8,128)S(1)}) custom-call(f32[128,2048]{1,0:T(8,128)S(1)} %get-tuple-element.26.blocks, s32[1,2048]{1,0:T(1,128)S(1)} %bitcast.8, s32[1,2048]{1,0:T(1,128)S(1)} %bitcast.11), custom_call_target="tpu_custom_call" | custom-call | flops 2147483648 | bytes 2097152 | tf_op jit(solution)/shard_map/walls/pallas_call | solution.py:425
  22.9 0.0 collective-permute-done.below
  22.9 0.0 collective-permute-done.1.above
  23.0 1.0 %collective-permute-start.4 = (f32[512,128]{1,0:T(8,128)S(1)}, f32[512,128]{1,0:T(8,128)S(1)}, u32[]{:S(2)}, u32[]{:S(2)}) collective-permute-start(f32[512,128]{1,0:T(8,128)S(1)} %get-tuple-element.43), channel_id=1, source_target_pairs={{0,16},{16,0},{32,48},{48,32},{64,80},{80,64},{96,112},{112,96},{1... | collective-permute-start | bytes 786440 | tf_op jit(solution)/shard_map/ppermute | solution.py:436
  24.0 1.3 %collective-permute-start.5 = (f32[512,128]{1,0:T(8,128)S(1)}, f32[512,128]{1,0:T(8,128)S(1)}, u32[]{:S(2)}, u32[]{:S(2)}) collective-permute-start(f32[512,128]{1,0:T(8,128)S(1)} %get-tuple-element.44), channel_id=1, source_target_pairs={{0,32},{16,48},{32,0},{48,16},{64,96},{80,112},{96,64},{112,80},{1... | collective-permute-start | bytes 786440 | tf_op jit(solution)/shard_map/ppermute | solution.py:436
  25.3 0.4 collective-permute-start.6
  25.7 0.0 copy-done.1
  25.7 0.0 copy-done.2
  25.7 0.0 copy-done.3
  25.7 0.0 copy-done.6
  25.7 5.6 %apply.1 = (f32[48,128]{1,0:T(8,128)S(1)}, f32[48,128]{1,0:T(8,128)S(1)}, f32[48,128]{1,0:T(8,128)S(1)}, f32[3,256]{1,0:T(4,128)S(1)}, f32[3,256]{1,0:T(4,128)S(1)}) custom-call(f32[96,128]{1,0:T(8,128)S(1)} %get-tuple-element.25.field, f32[6,256]{1,0:T(8,128)S(1)} %collective-permute-done.below, f32[6,256]{1,0:T(8,128)S(1)} %collective-permute-done.1.above, ...), custom_call_target="tpu_custom_call" | custom-call | flops 805306368 | bytes 196608 | tf_op jit(solution)/shard_map/apply/pallas_call | solution.py:380
  31.4 0.0 collective-permute-start.2
  31.4 4.8 %collective-permute-start.3 = (f32[3,256]{1,0:T(4,128)S(1)}, f32[3,256]{1,0:T(4,128)S(1)}, u32[]{:S(2)}, u32[]{:S(2)}) collective-permute-start(f32[3,256]{1,0:T(4,128)S(1)} %get-tuple-element.40), channel_id=1, source_target_pairs={{0,15},{1,0},{2,1},{3,2},{4,3},{5,4},{6,5},{7,6},{8,7},{9,8},{10,9... | collective-permute-start | bytes 9224 | tf_op jit(solution)/shard_map/ppermute | solution.py:391
  36.2 1.4 %local.1 = (f32[48,128]{1,0:T(8,128)S(1)}, f32[128,256]{1,0:T(8,128)S(1)}) custom-call(f32[48,128]{1,0:T(8,128)S(1)} %get-tuple-element.35.base, f32[48,128]{1,0:T(8,128)S(1)} %get-tuple-element.36.scale, f32[48,128]{1,0:T(8,128)S(1)} %get-tuple-element.37.applied, s32[4,8192]{1,0:T(4,128)S(1)} %copy-done.1, s32[1,2048]{1,0:T(1,128)S(1)} %bitcast.9, ...), custom_call_target="tpu_custom_call" | custom-call | flops 786432000 | bytes 2097152 | tf_op jit(solution)/shard_map/local/pallas_call | solution.py:448
  37.6 0.0 copy-start
  37.6 0.0 collective-permute-done.2.below
  37.6 0.0 collective-permute-done.3.above
  37.6 0.0 collective-permute-done.4.rest_1_
  37.6 0.0 collective-permute-done.5.rest_2_
  37.7 0.3 collective-permute-done.6.rest_3_
  37.9 1.2 %rims.1 = (f32[3,2048]{1,0:T(4,128)}, f32[128,8,128]{2,1,0:T(8,128)S(1)}) custom-call(f32[48,128]{1,0:T(8,128)S(1)} %get-tuple-element.38.local, f32[48,128]{1,0:T(8,128)S(1)} %get-tuple-element.36.scale, f32[3,256]{1,0:T(4,128)S(1)} %collective-permute-done.2.below, f32[3,256]{1,0:T(4,128)S(1)} %collective-permute-done.3.above, s32[4,8192]{1,0:T(4,128)S(1)} %copy-done.1, ...), custom_call_target="tpu_custom_call" | custom-call | flops 786432000 | bytes 2097152 | tf_op jit(solution)/shard_map/rims/pallas_call | solution.py:460
  39.1 22.6 %all_to_all.5.got = f32[128,8,128]{2,1,0:T(8,128)S(1)} all-to-all(f32[128,8,128]{2,1,0:T(8,128)S(1)} %get-tuple-element.46), channel_id=1, replica_groups=mesh['dom'=8,'sub'=16] {'dom','sub'}, dimensions={0} | all-to-all | bytes 1048576 | tf_op jit(solution)/shard_map/all_to_all | solution.py:474
  61.7 1.1 %owners.1 = f32[16,128]{1,0:T(8,128)} custom-call(f32[128,8,128]{2,1,0:T(8,128)S(1)} %all_to_all.5.got, bf16[12,128]{1,0:T(8,128)(2,1)S(1)} %copy-done), custom_call_target="tpu_custom_call" | custom-call | flops 1000000 | bytes 524288 | tf_op jit(solution)/shard_map/owners/pallas_call | solution.py:475
  (3 shorter events, 0.0 us)
Async XLA Ops:
  0.6 19.9 %copy-start.4 = (s32[2048,1]{0,1:T(1,128)S(1)}, s32[2048,1]{0,1:T(1,128)}, u32[]{:S(2)}) copy-start(s32[2048,1]{0,1:T(1,128)} %param.20) | copy-start | bytes 24580
  0.6 19.9 %copy-start.5 = (s32[2048]{0:T(1024)S(1)}, s32[2048]{0:T(1024)}, u32[]{:S(2)}) copy-start(s32[2048]{0:T(1024)} %param.21) | copy-start | bytes 24580
  13.6 9.3 %collective-permute-start = (f32[6,256]{1,0:T(8,128)S(1)}, f32[6,256]{1,0:T(8,128)S(1)}, u32[]{:S(2)}, u32[]{:S(2)}) collective-permute-start(f32[6,256]{1,0:T(8,128)S(1)} %get-tuple-element.31), channel_id=1, source_target_pairs={{0,1},{1,2},{2,3},{3,4},{4,5},{5,6},{6,7},{7,8},{8,9},{9,10},{10,1... | collective-permute-start | bytes 18440 | tf_op jit(solution)/shard_map/ppermute | solution.py:390
  16.1 6.8 %collective-permute-start.1 = (f32[6,256]{1,0:T(8,128)S(1)}, f32[6,256]{1,0:T(8,128)S(1)}, u32[]{:S(2)}, u32[]{:S(2)}) collective-permute-start(f32[6,256]{1,0:T(8,128)S(1)} %get-tuple-element.32), channel_id=1, source_target_pairs={{0,15},{1,0},{2,1},{3,2},{4,3},{5,4},{6,5},{7,6},{8,7},{9,8},{10,9... | collective-permute-start | bytes 18440 | tf_op jit(solution)/shard_map/ppermute | solution.py:391
  20.5 5.2 %copy-start.1 = (s32[4,8192]{1,0:T(4,128)S(1)}, s32[4,8192]{1,0:T(4,128)}, u32[]{:S(2)}) copy-start(s32[4,8192]{1,0:T(4,128)} %conn.5) | copy-start | bytes 393220
  20.5 5.2 %copy-start.2 = (f32[8192]{0:T(1024)S(1)}, f32[8192]{0:T(1024)}, u32[]{:S(2)}) copy-start(f32[8192]{0:T(1024)} %param.17) | copy-start | bytes 98308
  20.5 5.2 %copy-start.3 = (f32[12,12]{1,0:T(8,128)S(1)}, f32[12,12]{1,0:T(8,128)}, u32[]{:S(2)}) copy-start(f32[12,12]{1,0:T(8,128)} %ref.1) | copy-start | bytes 1732
  20.6 5.2 %copy-start.6 = (s32[1,1,256]{2,1,0:T(1,128)S(1)}, s32[1,1,256]{2,1,0:T(1,128)}, u32[]{:S(2)}) copy-start(s32[1,1,256]{2,1,0:T(1,128)} %param.19) | copy-start | bytes 3076
  23.0 14.7 %collective-permute-start.4 = (f32[512,128]{1,0:T(8,128)S(1)}, f32[512,128]{1,0:T(8,128)S(1)}, u32[]{:S(2)}, u32[]{:S(2)}) collective-permute-start(f32[512,128]{1,0:T(8,128)S(1)} %get-tuple-element.43), channel_id=1, source_target_pairs={{0,16},{16,0},{32,48},{48,32},{64,80},{80,64},{96,112},{112,96},{1... | collective-permute-start | bytes 786440 | tf_op jit(solution)/shard_map/ppermute | solution.py:436
  24.0 13.7 %collective-permute-start.5 = (f32[512,128]{1,0:T(8,128)S(1)}, f32[512,128]{1,0:T(8,128)S(1)}, u32[]{:S(2)}, u32[]{:S(2)}) collective-permute-start(f32[512,128]{1,0:T(8,128)S(1)} %get-tuple-element.44), channel_id=1, source_target_pairs={{0,32},{16,48},{32,0},{48,16},{64,96},{80,112},{96,64},{112,80},{1... | collective-permute-start | bytes 786440 | tf_op jit(solution)/shard_map/ppermute | solution.py:436
  25.3 12.6 %collective-permute-start.6 = (f32[512,128]{1,0:T(8,128)S(1)}, f32[512,128]{1,0:T(8,128)S(1)}, u32[]{:S(2)}, u32[]{:S(2)}) collective-permute-start(f32[512,128]{1,0:T(8,128)S(1)} %get-tuple-element.45), channel_id=1, source_target_pairs={{0,48},{16,32},{32,16},{48,0},{64,112},{80,96},{96,80},{112,64},{1... | collective-permute-start | bytes 786440 | tf_op jit(solution)/shard_map/ppermute | solution.py:436
  31.4 6.3 %collective-permute-start.2 = (f32[3,256]{1,0:T(4,128)S(1)}, f32[3,256]{1,0:T(4,128)S(1)}, u32[]{:S(2)}, u32[]{:S(2)}) collective-permute-start(f32[3,256]{1,0:T(4,128)S(1)} %get-tuple-element.39), channel_id=1, source_target_pairs={{0,1},{1,2},{2,3},{3,4},{4,5},{5,6},{6,7},{7,8},{8,9},{9,10},{10,1... | collective-permute-start | bytes 9224 | tf_op jit(solution)/shard_map/ppermute | solution.py:390
  31.4 6.3 %collective-permute-start.3 = (f32[3,256]{1,0:T(4,128)S(1)}, f32[3,256]{1,0:T(4,128)S(1)}, u32[]{:S(2)}, u32[]{:S(2)}) collective-permute-start(f32[3,256]{1,0:T(4,128)S(1)} %get-tuple-element.40), channel_id=1, source_target_pairs={{0,15},{1,0},{2,1},{3,2},{4,3},{5,4},{6,5},{7,6},{8,7},{9,8},{10,9... | collective-permute-start | bytes 9224 | tf_op jit(solution)/shard_map/ppermute | solution.py:391
  37.6 24.1 %copy-start = (bf16[12,128]{1,0:T(8,128)(2,1)S(1)}, bf16[12,128]{1,0:T(8,128)(2,1)}, u32[]{:S(2)}) copy-start(bf16[12,128]{1,0:T(8,128)(2,1)} %w_adjoint.1) | copy-start | bytes 9220

commit v3 on v2

--- a/solution.py
+++ b/solution.py
@@ -15,7 +15,7 @@
 GROUP = 4
 KEPT = PATCH_DEV // GROUP
 FRONT_VMEM = 40
-ROWS = 8
+ROWS = KEPT + 2
 
 mass_shift = 0.5
 relax = 0.7
@@ -102,7 +102,8 @@
 def front_kernel(*refs, walls):
     sources, (field, up, low, blocks), held, sems = refs[:11], refs[11:15], refs[15:26], refs[26]
     traces, states, jac, stiff, conn, w_trace, w_state, w_node, w_block, perm, ref = held
-    spans = [slice(s, s + walls) for s in range(0, traces.shape[1], walls)]
+    cuts = [0, walls // 4, *range(walls, traces.shape[1] + 1, walls)]
+    spans = [slice(p, q) for p, q in zip(cuts, cuts[1:])]
     copies = []
 
     def fetch(k, span=None):
@@ -127,8 +128,7 @@
     node_t = jnp.concatenate([w_node[...].astype(f32), pad], axis=0).astype(bf16)
     block_t = w_block[...].astype(f32).T.astype(bf16)
     cut = FIELDS * HIS
-    sens = jnp.zeros((cut, LANES), f32)
-    weight = [jnp.zeros((HIS, LANES), f32) for _ in range(4)]
+    sums = [jnp.zeros((LANES, 2 * (cut + HIS)), f32) for _ in range(4)]
     for s, span in enumerate(spans):
         for copy in first if s == 0 else later[s - 1]:
             copy.wait()
@@ -136,8 +136,9 @@
         tangent = mxu(state_t, states[:, span], NN)
         product = (jac[:, span] * upsilon * tangent).astype(bf16)
         terms = mxu(node_t, product, NN)
+        if s < 2:
+            blocks[:, span] = mxu(block_t, product, NN)
         if s == 0:
-            blocks[...] = mxu(block_t, product, NN)
             for copy in small:
                 copy.wait()
         top, rest = halves(terms)
@@ -148,18 +149,19 @@
             rows = [top[c * 4 + a : c * 4 + a + 1] for c in range(FIELDS)] + [stiff_top]
             rows += [rest[c * 4 + a : c * 4 + a + 1] for c in range(FIELDS)] + [stiff_rest]
             spread = placed(high[a : a + 1], rows)
-            out = mxu(spread, one_hot(lane[a : a + 1], LANES), NT)
-            sens += out[:cut] + out[cut + HIS : 2 * cut + HIS]
-            weight[a] += out[cut : cut + HIS] + out[2 * cut + HIS :]
+            sums[a] += mxu(one_hot(lane[a : a + 1], LANES), spread, NT)
 
     for copy in last:
         copy.wait()
+    sums = [x.T for x in sums]
+    sums = [x[: cut + HIS] + x[cut + HIS :] for x in sums]
+    sens = sums[0][:cut] + sums[1][:cut] + sums[2][:cut] + sums[3][:cut]
     diag = []
     for c in range(FIELDS):
         total = jnp.zeros((HIS, LANES), f32)
         for a in range(4):
             i = c * 4 + a
-            total += ref[i : i + 1, i : i + 1] * weight[a]
+            total += ref[i : i + 1, i : i + 1] * sums[a][cut:]
         diag.append(total)
     both = jnp.concatenate([sens] + diag, axis=0)
     field[...] = both
@@ -298,10 +300,10 @@
     kept = pieces[0][...]
     for piece in pieces[1:]:
         kept += piece[...]
-    payload[:, :KEPT, :] = kept.reshape(owners, KEPT, LANES)
-    payload[:, KEPT : KEPT + 1, :] = total[:, :LANES].reshape(owners, 1, LANES)
-    payload[:, KEPT + 1 : KEPT + 2, :] = total[:, LANES:].reshape(owners, 1, LANES)
-    payload[:, KEPT + 2 :, :] = jnp.zeros((owners, ROWS - KEPT - 2, LANES), f32)
+    kept = kept.reshape(owners, KEPT, LANES)
+    for k in range(2):
+        rows = [kept[:, r, :] for r in range(k, KEPT, 2)] + [total[:, k * LANES : (k + 1) * LANES]]
+        payload[:, k : k + 1, :] = jnp.concatenate(rows, axis=1).reshape(owners, 1, ROWS // 2 * LANES)
 
 
 def owner_kernel(got, w_adjoint, out):
@@ -318,16 +320,17 @@
         total = by_dom[g]
         for d in range(g + GROUP, doms, GROUP):
             total += by_dom[d]
-        parts.append(total[:KEPT])
+        parts += [total[r % 2 : r % 2 + 1, r // 2 * LANES : (r // 2 + 1) * LANES] for r in range(KEPT)]
     everything = by_dom[0]
     for d in range(1, doms):
         everything += by_dom[d]
+    everything = everything[:, KEPT // 2 * LANES :]
     shape = (PATCH_DEV, LANES)
     mine = lax.broadcasted_iota(jnp.int32, shape, 1) % PATCH_DEV == lax.broadcasted_iota(
         jnp.int32, shape, 0
     )
     spread = [
-        jnp.where(mine, everything[KEPT + k : KEPT + k + 1], 0.0) for k in range(2)
+        jnp.where(mine, everything[k : k + 1], 0.0) for k in range(2)
     ]
     shape = (2 * LANES, w_adjoint.shape[0])
     rows = lax.broadcasted_iota(jnp.int32, shape, 0) // PATCH_DEV
@@ -359,7 +362,7 @@
     trace, elements = fetched[0].shape
     quad, width = fetched[8].shape
     outs = [shape(2 * FIELDS * HIS, LANES), shape(6, RIM), shape(6, RIM), shape(width, walls)]
-    copies = len(fetched) + 2 * (elements // walls - 1)
+    copies = len(fetched) + 2 * (elements // walls)
     return pl.pallas_call(
         functools.partial(front_kernel, walls=walls),
         in_specs=[pl.BlockSpec(memory_space=pl.ANY)] * len(fetched),
@@ -465,8 +468,8 @@
             whole(owner.shape), whole(patch.shape), whole(perm.shape), whole(sums.shape),
             *[whole(pieces[0].shape)] * GROUP,
         ],
-        out_specs=[whole((FIELDS, HIS * LANES)), whole((devices, ROWS, LANES))],
-        out_shape=[shape(FIELDS, HIS * LANES), shape(devices, ROWS, LANES)],
+        out_specs=[whole((FIELDS, HIS * LANES)), whole((devices, 2, ROWS // 2 * LANES))],
+        out_shape=[shape(FIELDS, HIS * LANES), shape(devices, 2, ROWS // 2 * LANES)],
         name="rims",
         **params(3000 * walls * LANES, 8 * devices * PATCH_DEV * width),
     )(local, scale, below, above, connect, owner, patch, perm, sums, *pieces)

time: 62.9 us -> 58.3 us (0.927)
  Pallas kernels: 24.6 us -> 21.3 us
  blocking collectives: 22.6 us -> 21.3 us
    pallas_call x1, Pallas kernels: 12.9 us -> 9.09 us  [front(): pl.pallas_call(functools.partial(front_kernel, walls=walls), in_specs=[pl...]
    all_to_all x1, blocking collectives: 22.6 us -> 21.3 us  [per_device(): lax.all_to_all(payload, ('dom', 'sub'), split_axis=0, concat_axis=0, tile...]
  transfers between devices with their start and end apart: 7 -> 7, of which waited for: 1 -> 1; matrix products, arithmetic and copies ran while one was open for 0% -> 0% of each run, Pallas kernels for 15% -> 16%
where the time goes in v3:
time: 58.3 us; the launch traced here: 58.2 us
  Pallas kernels  21.3 us (37%)
  blocking collectives  21.3 us (37%)
  starting transfers between devices  14.5 us (25%)
  between operations  0.76 us (1%)
    all_to_all x1, blocking collectives, per_device(): lax.all_to_all(payload, ('dom', 'sub'), split_axis=0, concat_axis=0, tile...  21.3 us
    ppermute x2, starting transfers between devices, exchanged(): lax.ppermute(low, 'sub', [(i, (i - 1) % count) for i in range(count)])  9.19 us
    pallas_call x1, Pallas kernels, front(): pl.pallas_call(functools.partial(front_kernel, walls=walls), in_specs=[pl...  9.09 us
    pallas_call x1, Pallas kernels, apply(): pl.pallas_call(functools.partial(apply_kernel, chunk=512), out_shape=[sma...  5.64 us
    ppermute x3, starting transfers between devices, per_device(): lax.ppermute(pieces[k], 'dom', [(i, i ^ k) for i in range(doms)])  2.76 us
    ppermute x2, starting transfers between devices, exchanged(): lax.ppermute(up, 'sub', [(i, (i + 1) % count) for i in range(count)])  2.54 us
    pallas_call x1, Pallas kernels, per_device(): pl.pallas_call(wall_kernel, out_shape=[shape(devices * KEPT, width)] * GR...  2.36 us
    pallas_call x1, Pallas kernels, per_device(): pl.pallas_call(rim_kernel, grid=(1,), in_specs=[*[whole(small.shape)] * 2...  1.71 us
  transfers between devices with their start and end apart: 7, of which 1 were waited for; matrix products, arithmetic and copies ran while one was open for 0% of the time, Pallas kernels for 16%

profile of v3, /device:TPU:1, one launch (start us, length us, event | category | flops | bytes accessed | tf_op | source)
XLA Modules:
  0.0 58.2 jit_solution(328636552471443122)
XLA Ops:
  0.6 0.0 copy-start.4
  0.6 0.0 copy-start.5
  0.7 9.1 %front.1 = (f32[96,128]{1,0:T(8,128)S(1)}, f32[6,256]{1,0:T(8,128)S(1)}, f32[6,256]{1,0:T(8,128)S(1)}, f32[128,2048]{1,0:T(8,128)S(1)}) custom-call(bf16[144,8192]{1,0:T(8,128)(2,1)} %refs_0_.1, bf16[144,8192]{1,0:T(8,128)(2,1)} %refs_1_.1, f32[1,8192]{1,0:T(1,128)} %bitcast.17, f32[1,8192]{1,0:T(1,128)} %bitcast.6, s32[4,8192]{1,0:T(4,128)} %conn.5, ...), custom_call_target="tpu_custom_call" | custom-call | flops 1811939328 | bytes 4718592 | tf_op jit(solution)/shard_map/front/pallas_call | solution.py:366
  9.8 2.5 %collective-permute-start = (f32[6,256]{1,0:T(8,128)S(1)}, f32[6,256]{1,0:T(8,128)S(1)}, u32[]{:S(2)}, u32[]{:S(2)}) collective-permute-start(f32[6,256]{1,0:T(8,128)S(1)} %get-tuple-element.31), channel_id=1, source_target_pairs={{0,1},{1,2},{2,3},{3,4},{4,5},{5,6},{6,7},{7,8},{8,9},{9,10},{10,1... | collective-permute-start | bytes 18440 | tf_op jit(solution)/shard_map/ppermute | solution.py:393
  12.3 4.4 %collective-permute-start.1 = (f32[6,256]{1,0:T(8,128)S(1)}, f32[6,256]{1,0:T(8,128)S(1)}, u32[]{:S(2)}, u32[]{:S(2)}) collective-permute-start(f32[6,256]{1,0:T(8,128)S(1)} %get-tuple-element.32), channel_id=1, source_target_pairs={{0,15},{1,0},{2,1},{3,2},{4,3},{5,4},{6,5},{7,6},{8,7},{9,8},{10,9... | collective-permute-start | bytes 18440 | tf_op jit(solution)/shard_map/ppermute | solution.py:394
  16.7 0.0 copy-done.4
  16.7 0.0 copy-done.5
  16.7 0.0 copy-start.3
  16.7 0.0 copy-start.6
  16.7 2.4 %walls.1 = (f32[512,128]{1,0:T(8,128)S(1)}, f32[512,128]{1,0:T(8,128)S(1)}, f32[512,128]{1,0:T(8,128)S(1)}, f32[512,128]{1,0:T(8,128)S(1)}) custom-call(f32[128,2048]{1,0:T(8,128)S(1)} %get-tuple-element.26.blocks, s32[1,2048]{1,0:T(1,128)S(1)} %bitcast.8, s32[1,2048]{1,0:T(1,128)S(1)} %bitcast.11), custom_call_target="tpu_custom_call" | custom-call | flops 2147483648 | bytes 2097152 | tf_op jit(solution)/shard_map/walls/pallas_call | solution.py:428
  19.1 0.0 collective-permute-done.below
  19.1 0.0 collective-permute-done.1.above
  19.1 1.0 %collective-permute-start.4 = (f32[512,128]{1,0:T(8,128)S(1)}, f32[512,128]{1,0:T(8,128)S(1)}, u32[]{:S(2)}, u32[]{:S(2)}) collective-permute-start(f32[512,128]{1,0:T(8,128)S(1)} %get-tuple-element.43), channel_id=1, source_target_pairs={{0,16},{16,0},{32,48},{48,32},{64,80},{80,64},{96,112},{112,96},{1... | collective-permute-start | bytes 786440 | tf_op jit(solution)/shard_map/ppermute | solution.py:439
  20.1 1.3 %collective-permute-start.5 = (f32[512,128]{1,0:T(8,128)S(1)}, f32[512,128]{1,0:T(8,128)S(1)}, u32[]{:S(2)}, u32[]{:S(2)}) collective-permute-start(f32[512,128]{1,0:T(8,128)S(1)} %get-tuple-element.44), channel_id=1, source_target_pairs={{0,32},{16,48},{32,0},{48,16},{64,96},{80,112},{96,64},{112,80},{1... | collective-permute-start | bytes 786440 | tf_op jit(solution)/shard_map/ppermute | solution.py:439
  21.5 0.4 collective-permute-start.6
  21.9 0.0 copy-done.1
  21.9 0.0 copy-done.2
  21.9 0.0 copy-done.3
  21.9 0.0 copy-done.6
  21.9 5.6 %apply.1 = (f32[48,128]{1,0:T(8,128)S(1)}, f32[48,128]{1,0:T(8,128)S(1)}, f32[48,128]{1,0:T(8,128)S(1)}, f32[3,256]{1,0:T(4,128)S(1)}, f32[3,256]{1,0:T(4,128)S(1)}) custom-call(f32[96,128]{1,0:T(8,128)S(1)} %get-tuple-element.25.field, f32[6,256]{1,0:T(8,128)S(1)} %collective-permute-done.below, f32[6,256]{1,0:T(8,128)S(1)} %collective-permute-done.1.above, ...), custom_call_target="tpu_custom_call" | custom-call | flops 805306368 | bytes 196608 | tf_op jit(solution)/shard_map/apply/pallas_call | solution.py:383
  27.5 0.0 collective-permute-start.2
  27.5 4.8 %collective-permute-start.3 = (f32[3,256]{1,0:T(4,128)S(1)}, f32[3,256]{1,0:T(4,128)S(1)}, u32[]{:S(2)}, u32[]{:S(2)}) collective-permute-start(f32[3,256]{1,0:T(4,128)S(1)} %get-tuple-element.40), channel_id=1, source_target_pairs={{0,15},{1,0},{2,1},{3,2},{4,3},{5,4},{6,5},{7,6},{8,7},{9,8},{10,9... | collective-permute-start | bytes 9224 | tf_op jit(solution)/shard_map/ppermute | solution.py:394
  32.3 1.4 %local.1 = (f32[48,128]{1,0:T(8,128)S(1)}, f32[128,256]{1,0:T(8,128)S(1)}) custom-call(f32[48,128]{1,0:T(8,128)S(1)} %get-tuple-element.35.base, f32[48,128]{1,0:T(8,128)S(1)} %get-tuple-element.36.scale, f32[48,128]{1,0:T(8,128)S(1)} %get-tuple-element.37.applied, s32[4,8192]{1,0:T(4,128)S(1)} %copy-done.1, s32[1,2048]{1,0:T(1,128)S(1)} %bitcast.9, ...), custom_call_target="tpu_custom_call" | custom-call | flops 786432000 | bytes 2097152 | tf_op jit(solution)/shard_map/local/pallas_call | solution.py:451
  33.8 0.0 copy-start
  33.8 0.0 collective-permute-done.2.below
  33.8 0.0 collective-permute-done.3.above
  33.8 0.0 collective-permute-done.4.rest_1_
  33.8 0.0 collective-permute-done.5.rest_2_
  33.8 0.3 collective-permute-done.6.rest_3_
  34.1 1.7 %rims.1 = (f32[3,2048]{1,0:T(4,128)}, f32[128,2,384]{2,1,0:T(2,128)S(1)}) custom-call(f32[48,128]{1,0:T(8,128)S(1)} %get-tuple-element.38.local, f32[48,128]{1,0:T(8,128)S(1)} %get-tuple-element.36.scale, f32[3,256]{1,0:T(4,128)S(1)} %collective-permute-done.2.below, f32[3,256]{1,0:T(4,128)S(1)} %collective-permute-done.3.above, s32[4,8192]{1,0:T(4,128)S(1)} %copy-done.1, ...), custom_call_target="tpu_custom_call" | custom-call | flops 786432000 | bytes 2097152 | tf_op jit(solution)/shard_map/rims/pallas_call | solution.py:463
  35.8 21.3 %all_to_all.5.got = f32[128,2,384]{2,1,0:T(2,128)S(1)} all-to-all(f32[128,2,384]{2,1,0:T(2,128)S(1)} %get-tuple-element.46), channel_id=1, replica_groups=mesh['dom'=8,'sub'=16] {'dom','sub'}, dimensions={0} | all-to-all | bytes 786432 | tf_op jit(solution)/shard_map/all_to_all | solution.py:477
  57.1 1.1 %owners.1 = f32[16,128]{1,0:T(8,128)} custom-call(f32[128,2,384]{2,1,0:T(2,128)S(1)} %all_to_all.5.got, bf16[12,128]{1,0:T(8,128)(2,1)S(1)} %copy-done), custom_call_target="tpu_custom_call" | custom-call | flops 1000000 | bytes 393216 | tf_op jit(solution)/shard_map/owners/pallas_call | solution.py:478
  (3 shorter events, 0.0 us)
Async XLA Ops:
  0.6 16.1 %copy-start.4 = (s32[2048,1]{0,1:T(1,128)S(1)}, s32[2048,1]{0,1:T(1,128)}, u32[]{:S(2)}) copy-start(s32[2048,1]{0,1:T(1,128)} %param.20) | copy-start | bytes 24580
  0.6 16.0 %copy-start.5 = (s32[2048]{0:T(1024)S(1)}, s32[2048]{0:T(1024)}, u32[]{:S(2)}) copy-start(s32[2048]{0:T(1024)} %param.21) | copy-start | bytes 24580
  9.8 9.3 %collective-permute-start = (f32[6,256]{1,0:T(8,128)S(1)}, f32[6,256]{1,0:T(8,128)S(1)}, u32[]{:S(2)}, u32[]{:S(2)}) collective-permute-start(f32[6,256]{1,0:T(8,128)S(1)} %get-tuple-element.31), channel_id=1, source_target_pairs={{0,1},{1,2},{2,3},{3,4},{4,5},{5,6},{6,7},{7,8},{8,9},{9,10},{10,1... | collective-permute-start | bytes 18440 | tf_op jit(solution)/shard_map/ppermute | solution.py:393
  12.3 6.8 %collective-permute-start.1 = (f32[6,256]{1,0:T(8,128)S(1)}, f32[6,256]{1,0:T(8,128)S(1)}, u32[]{:S(2)}, u32[]{:S(2)}) collective-permute-start(f32[6,256]{1,0:T(8,128)S(1)} %get-tuple-element.32), channel_id=1, source_target_pairs={{0,15},{1,0},{2,1},{3,2},{4,3},{5,4},{6,5},{7,6},{8,7},{9,8},{10,9... | collective-permute-start | bytes 18440 | tf_op jit(solution)/shard_map/ppermute | solution.py:394
  16.7 5.2 %copy-start.1 = (s32[4,8192]{1,0:T(4,128)S(1)}, s32[4,8192]{1,0:T(4,128)}, u32[]{:S(2)}) copy-start(s32[4,8192]{1,0:T(4,128)} %conn.5) | copy-start | bytes 393220
  16.7 5.2 %copy-start.2 = (f32[8192]{0:T(1024)S(1)}, f32[8192]{0:T(1024)}, u32[]{:S(2)}) copy-start(f32[8192]{0:T(1024)} %param.17) | copy-start | bytes 98308
  16.7 5.2 %copy-start.3 = (f32[12,12]{1,0:T(8,128)S(1)}, f32[12,12]{1,0:T(8,128)}, u32[]{:S(2)}) copy-start(f32[12,12]{1,0:T(8,128)} %ref.1) | copy-start | bytes 1732
  16.7 5.2 %copy-start.6 = (s32[1,1,256]{2,1,0:T(1,128)S(1)}, s32[1,1,256]{2,1,0:T(1,128)}, u32[]{:S(2)}) copy-start(s32[1,1,256]{2,1,0:T(1,128)} %param.19) | copy-start | bytes 3076
  19.1 14.7 %collective-permute-start.4 = (f32[512,128]{1,0:T(8,128)S(1)}, f32[512,128]{1,0:T(8,128)S(1)}, u32[]{:S(2)}, u32[]{:S(2)}) collective-permute-start(f32[512,128]{1,0:T(8,128)S(1)} %get-tuple-element.43), channel_id=1, source_target_pairs={{0,16},{16,0},{32,48},{48,32},{64,80},{80,64},{96,112},{112,96},{1... | collective-permute-start | bytes 786440 | tf_op jit(solution)/shard_map/ppermute | solution.py:439
  20.1 13.7 %collective-permute-start.5 = (f32[512,128]{1,0:T(8,128)S(1)}, f32[512,128]{1,0:T(8,128)S(1)}, u32[]{:S(2)}, u32[]{:S(2)}) collective-permute-start(f32[512,128]{1,0:T(8,128)S(1)} %get-tuple-element.44), channel_id=1, source_target_pairs={{0,32},{16,48},{32,0},{48,16},{64,96},{80,112},{96,64},{112,80},{1... | collective-permute-start | bytes 786440 | tf_op jit(solution)/shard_map/ppermute | solution.py:439
  21.5 12.6 %collective-permute-start.6 = (f32[512,128]{1,0:T(8,128)S(1)}, f32[512,128]{1,0:T(8,128)S(1)}, u32[]{:S(2)}, u32[]{:S(2)}) collective-permute-start(f32[512,128]{1,0:T(8,128)S(1)} %get-tuple-element.45), channel_id=1, source_target_pairs={{0,48},{16,32},{32,16},{48,0},{64,112},{80,96},{96,80},{112,64},{1... | collective-permute-start | bytes 786440 | tf_op jit(solution)/shard_map/ppermute | solution.py:439
  27.5 6.3 %collective-permute-start.2 = (f32[3,256]{1,0:T(4,128)S(1)}, f32[3,256]{1,0:T(4,128)S(1)}, u32[]{:S(2)}, u32[]{:S(2)}) collective-permute-start(f32[3,256]{1,0:T(4,128)S(1)} %get-tuple-element.39), channel_id=1, source_target_pairs={{0,1},{1,2},{2,3},{3,4},{4,5},{5,6},{6,7},{7,8},{8,9},{9,10},{10,1... | collective-permute-start | bytes 9224 | tf_op jit(solution)/shard_map/ppermute | solution.py:393
  27.5 6.3 %collective-permute-start.3 = (f32[3,256]{1,0:T(4,128)S(1)}, f32[3,256]{1,0:T(4,128)S(1)}, u32[]{:S(2)}, u32[]{:S(2)}) collective-permute-start(f32[3,256]{1,0:T(4,128)S(1)} %get-tuple-element.40), channel_id=1, source_target_pairs={{0,15},{1,0},{2,1},{3,2},{4,3},{5,4},{6,5},{7,6},{8,7},{9,8},{10,9... | collective-permute-start | bytes 9224 | tf_op jit(solution)/shard_map/ppermute | solution.py:394
  33.8 23.4 %copy-start = (bf16[12,128]{1,0:T(8,128)(2,1)S(1)}, bf16[12,128]{1,0:T(8,128)(2,1)}, u32[]{:S(2)}) copy-start(bf16[12,128]{1,0:T(8,128)(2,1)} %w_adjoint.1) | copy-start | bytes 9220

commit v4 on v3

--- a/solution.py
+++ b/solution.py
@@ -12,7 +12,8 @@
 HIS = 16
 FIELDS = 3
 RIM = 256
-GROUP = 4
+PIECES = 8
+GROUP = 2
 KEPT = PATCH_DEV // GROUP
 FRONT_VMEM = 40
 ROWS = KEPT + 2
@@ -99,9 +100,31 @@
     return jnp.concatenate(parts, axis=0)
 
 
+def write_message(message, rims, perm, conn, owner, patch):
+    message[:8] = jnp.concatenate([rims, perm[...].astype(f32), jnp.zeros((1, RIM), f32)], axis=0)
+    for i in range(PIECES):
+        cols = slice(i * RIM, (i + 1) * RIM)
+        message[8 + 4 * i : 12 + 4 * i] = conn[:, cols].astype(f32)
+        target = owner[:, cols] * PATCH_DEV + patch[:, cols]
+        message[8 + 4 * PIECES + i : 9 + 4 * PIECES + i] = target.astype(f32)
+
+
+def read_message(message):
+    pairs = range(PIECES // 2)
+    slots = jnp.concatenate([message[8 + 8 * j : 16 + 8 * j] for j in pairs], axis=1)
+    first = 8 + 4 * PIECES
+    targets = [
+        jnp.concatenate([message[first + 2 * j + k : first + 2 * j + k + 1] for j in pairs], axis=1)
+        for k in range(2)
+    ]
+    return slots.astype(jnp.int32), [x.astype(jnp.int32) for x in targets]
+
+
 def front_kernel(*refs, walls):
-    sources, (field, up, low, blocks), held, sems = refs[:11], refs[11:15], refs[15:26], refs[26]
-    traces, states, jac, stiff, conn, w_trace, w_state, w_node, w_block, perm, ref = held
+    count = (len(refs) - 5) // 2
+    sources, (field, up, low, blocks), held = refs[:count], refs[count : count + 4], refs[count + 4 : -1]
+    sems = refs[-1]
+    traces, states, jac, stiff, conn, w_trace, w_state, w_node, w_block, perm, ref, owner, patch = held
     cuts = [0, walls // 4, *range(walls, traces.shape[1] + 1, walls)]
     spans = [slice(p, q) for p, q in zip(cuts, cuts[1:])]
     copies = []
@@ -119,7 +142,7 @@
     first = [fetch(0, spans[0]), fetch(1, spans[0]), fetch(2)]
     small = [fetch(k) for k in (3, 4)]
     later = [[fetch(0, span), fetch(1, span)] for span in spans[1:]]
-    last = [fetch(k) for k in (9, 10)]
+    last = [fetch(k) for k in (9, 10, 11, 12)]
     for copy in weights:
         copy.wait()
     trace_t = w_trace[...].astype(f32).T.astype(bf16)
@@ -165,8 +188,8 @@
         diag.append(total)
     both = jnp.concatenate([sens] + diag, axis=0)
     field[...] = both
-    up[...] = rim_rows(both, HIS - 2)
-    low[...] = reorder(rim_rows(both, 0), perm[...], NN)
+    write_message(up, rim_rows(both, HIS - 2), perm, conn, owner, patch)
+    write_message(low, reorder(rim_rows(both, 0), perm[...], NN), perm, conn, owner, patch)
 
 
 def group_place():
@@ -175,7 +198,8 @@
 
 def wall_kernel(blocks, owner, patch, *sums):
     rows = sums[0].shape[0]
-    slot = (patch[...] // KEPT ^ group_place()) * rows + owner[...] * KEPT + patch[...] % KEPT
+    owners = rows // KEPT
+    slot = (patch[...] // KEPT ^ group_place()) * rows + patch[...] % KEPT * owners + owner[...]
     top, rest = halves(blocks[...])
     both = jnp.concatenate([top, rest], axis=0).astype(bf16)
     for k in range(GROUP):
@@ -183,17 +207,27 @@
         sums[k][...] = out[:, :LANES] + out[:, LANES:]
 
 
-def looked_up(table, slots, lines):
-    count = table.shape[0] // HIS
+def all_lines(table):
+    return [[(h, table[f * HIS + h : f * HIS + h + 1]) for h in range(HIS)] for f in range(FIELDS)]
+
+
+def rim_lines(rims, first):
+    return [
+        [(first + k, rims[f : f + 1, k * LANES : (k + 1) * LANES]) for k in range(2)]
+        for f in range(FIELDS)
+    ]
+
+
+def looked_up(table, slots):
     n = slots.shape[1] // LANES
-    rows = [[] for _ in range(count)]
+    rows = [[] for _ in table]
     for k in range(n):
         here = slots[:, k * LANES : (k + 1) * LANES]
         high, lane = here >> 7, here & (LANES - 1)
-        for f in range(count):
+        for f, lines in enumerate(table):
             got = jnp.zeros((8, LANES), f32)
-            for h in lines:
-                line = jnp.broadcast_to(table[f * HIS + h : f * HIS + h + 1], (8, LANES))
+            for h, line in lines:
+                line = jnp.broadcast_to(line, (8, LANES))
                 picked = jnp.take_along_axis(line, lane, axis=1, mode="promise_in_bounds")
                 got = jnp.where(high == h, picked, got)
             rows[f].append(got)
@@ -205,7 +239,7 @@
     base, scale, applied, up, low,
     *, chunk,
 ):
-    shared = field[...] + rims(below[...], above[...], perm[...])
+    shared = field[...] + rims(below[:6], above[:6], perm[...])
     cut = FIELDS * HIS
     sens, diag = shared[:cut], shared[cut:] + mass_shift
     over = relax / diag
@@ -235,7 +269,7 @@
         first = slice(start, start + chunk)
         second = slice(half + start, half + start + chunk)
         slots = jnp.concatenate([conn[:, first], conn[:, second]], axis=0)
-        values = jnp.concatenate(looked_up(psi, slots, range(HIS)), axis=0)
+        values = jnp.concatenate(looked_up(all_lines(psi), slots), axis=0)
         top, rest = halves(values)
         pushed = mxu(wide, jnp.concatenate([top, rest], axis=0).astype(bf16), NN)
         pushed = pushed[:24] + pushed[24:]
@@ -254,56 +288,58 @@
     low[...] = reorder(rim_rows(total, 0), perm[...], NN)
 
 
-def patch_sums(values, owner, patch, owners):
-    half = values[0].shape[1]
+def patch_sums(values, targets, owners):
     parts = [halves(v) for v in values]
     total = jnp.zeros((owners, 24 * PATCH_DEV), f32)
-    for k in range(2):
-        cols = slice(k * half, (k + 1) * half)
+    for k, target in enumerate(targets):
         rows = [
             parts[c][p][4 * k + a : 4 * k + a + 1]
             for p in range(2)
             for c in range(FIELDS)
             for a in range(4)
         ]
-        spread = placed(patch[:, cols], rows)
-        total += mxu(one_hot(owner[:, cols], owners), spread, NT)
+        spread = placed(target % PATCH_DEV, rows)
+        total += mxu(one_hot(target // PATCH_DEV, owners), spread, NT)
     return total[:, : 12 * PATCH_DEV] + total[:, 12 * PATCH_DEV :]
 
 
-def wall_slots(conn):
+def sums_kernel(base, scale, applied, below, above, conn, owner, patch, perm, *rest):
+    *pieces, payload = rest
+    owners = payload.shape[0]
+    change = scale[...] * applied[...]
+    psi = base[...] - change
     half = conn.shape[1] // 2
-    return jnp.concatenate([conn[:, :half], conn[:, half:]], axis=0)
-
-
-def local_kernel(base, scale, applied, conn, owner, patch, local, sums):
-    psi = base[...] - scale[...] * applied[...]
-    local[...] = psi
-    values = looked_up(psi, wall_slots(conn), range(HIS))
-    sums[:, : 12 * PATCH_DEV] = patch_sums(values, owner, patch, sums.shape[0])
-    sums[:, 12 * PATCH_DEV :] = jnp.zeros((sums.shape[0], 4 * PATCH_DEV), f32)
-
-
-def rim_kernel(
-    local, scale, below, above, conn, owner, patch, perm, sums, *rest
-):
-    *pieces, adjoint, payload = rest
-    change = -scale[...] * rims(below[...], above[...], perm[...])
-    psi = local[...] + change
+    slots = jnp.concatenate([conn[:, :half], conn[:, half:]], axis=0)
+    target = owner[...] * PATCH_DEV + patch[...]
+    values = looked_up(all_lines(psi), slots)
+    total = patch_sums(values, [target[:, :half], target[:, half:]], owners)
+
+    place = lax.axis_index("sub")
+    last = lax.axis_size("sub") - 1
+    lower = reorder(rim_rows(-change, 0), perm[...], NN)
+    lower = jnp.where(place == 0, 0.0, lower)
+    slots, targets = read_message(below)
+    total += patch_sums(looked_up(rim_lines(lower, HIS - 2), slots), targets, owners)
+    upper = reorder(rim_rows(-change, HIS - 2), above[6:7].astype(jnp.int32), NT)
+    upper = jnp.where(place == last, 0.0, upper)
+    slots, targets = read_message(above)
+    total += patch_sums(looked_up(rim_lines(upper, 0), slots), targets, owners)
+
+    total = jnp.concatenate([total, jnp.zeros((owners, 4 * PATCH_DEV), f32)], axis=1)
+    kept = pieces[0][...]
+    for piece in pieces[1:]:
+        kept += piece[...]
+    for k in range(2):
+        rows = [kept[r * owners : (r + 1) * owners] for r in range(k, KEPT, 2)]
+        rows.append(total[:, k * LANES : (k + 1) * LANES])
+        payload[:, k : k + 1, :] = jnp.concatenate(rows, axis=1).reshape(owners, 1, ROWS // 2 * LANES)
+
+
+def adjoint_kernel(base, scale, applied, below, above, perm, adjoint):
+    psi = base[...] - scale[...] * (applied[...] + rims(below[...], above[...], perm[...]))
     for c in range(FIELDS):
         for h in range(HIS):
             adjoint[c : c + 1, h * LANES : (h + 1) * LANES] = psi[c * HIS + h : c * HIS + h + 1]
-    values = looked_up(change, wall_slots(conn), (0, 1, HIS - 2, HIS - 1))
-    owners = sums.shape[0]
-    more = patch_sums(values, owner, patch, owners)
-    total = sums[...] + jnp.concatenate([more, jnp.zeros((owners, 4 * PATCH_DEV), f32)], axis=1)
-    kept = pieces[0][...]
-    for piece in pieces[1:]:
-        kept += piece[...]
-    kept = kept.reshape(owners, KEPT, LANES)
-    for k in range(2):
-        rows = [kept[:, r, :] for r in range(k, KEPT, 2)] + [total[:, k * LANES : (k + 1) * LANES]]
-        payload[:, k : k + 1, :] = jnp.concatenate(rows, axis=1).reshape(owners, 1, ROWS // 2 * LANES)
 
 
 def owner_kernel(got, w_adjoint, out):
@@ -361,7 +397,8 @@
 def front(walls, *fetched):
     trace, elements = fetched[0].shape
     quad, width = fetched[8].shape
-    outs = [shape(2 * FIELDS * HIS, LANES), shape(6, RIM), shape(6, RIM), shape(width, walls)]
+    message = shape(8 + 5 * PIECES, RIM)
+    outs = [shape(2 * FIELDS * HIS, LANES), message, message, shape(width, walls)]
     copies = len(fetched) + 2 * (elements // walls)
     return pl.pallas_call(
         functools.partial(front_kernel, walls=walls),
@@ -421,7 +458,7 @@
     perm = shared_perm.reshape(1, -1)
     field, up, low, blocks = front(
         walls, adjoint_traces, primal_traces, jac, stiff, connect,
-        w_trace, w_state, w_node.T, w_block, perm, stiff_ref,
+        w_trace, w_state, w_node.T, w_block, perm, stiff_ref, owner, patch,
     )
     below, above = exchanged(up, low)
 
@@ -445,36 +482,31 @@
     base, scale, applied, up, low = apply(
         field, below, above, connect, stiff, perm, stiff_ref
     )
-    below, above = exchanged(up, low)
-
     conn_spec = pl.BlockSpec((4, walls), lambda s: (0, 0))
-    local, sums = pl.pallas_call(
-        local_kernel,
+    payload = shape(devices, 2, ROWS // 2 * LANES)
+    payload = pl.pallas_call(
+        sums_kernel,
         grid=(1,),
         in_specs=[
-            *[whole(small.shape)] * 3, conn_spec, whole(owner.shape), whole(patch.shape),
-        ],
-        out_specs=[whole(small.shape), whole((devices, 2 * LANES))],
-        out_shape=[small, shape(devices, 2 * LANES)],
-        name="local",
-        **params(3000 * walls * LANES, 8 * devices * PATCH_DEV * width),
-    )(base, scale, applied, connect, owner, patch)
-
-    adjoint, payload = pl.pallas_call(
-        rim_kernel,
-        grid=(1,),
-        in_specs=[
-            *[whole(small.shape)] * 2, whole(below.shape), whole(above.shape), conn_spec,
-            whole(owner.shape), whole(patch.shape), whole(perm.shape), whole(sums.shape),
+            *[whole(small.shape)] * 3, *[whole(below.shape)] * 2, conn_spec,
+            whole(owner.shape), whole(patch.shape), whole(perm.shape),
             *[whole(pieces[0].shape)] * GROUP,
         ],
-        out_specs=[whole((FIELDS, HIS * LANES)), whole((devices, 2, ROWS // 2 * LANES))],
-        out_shape=[shape(FIELDS, HIS * LANES), shape(devices, 2, ROWS // 2 * LANES)],
-        name="rims",
+        out_specs=whole(payload.shape),
+        out_shape=payload,
+        name="sums",
         **params(3000 * walls * LANES, 8 * devices * PATCH_DEV * width),
-    )(local, scale, below, above, connect, owner, patch, perm, sums, *pieces)
-
+    )(base, scale, applied, below, above, connect, owner, patch, perm, *pieces)
+
+    payload, up, low = lax.optimization_barrier((payload, up, low))
     got = lax.all_to_all(payload, ("dom", "sub"), split_axis=0, concat_axis=0, tiled=True)
+    below, above = exchanged(up, low)
+    adjoint = pl.pallas_call(
+        adjoint_kernel,
+        out_shape=shape(FIELDS, HIS * LANES),
+        name="adjoint",
+        **params(10**7, 10**5),
+    )(base, scale, applied, below, above, perm)
     grad = pl.pallas_call(
         owner_kernel,
         out_shape=shape(PATCH_DEV, width),

time: 58.3 us -> 53.8 us (0.923)
  blocking collectives: 21.3 us -> 0 us
  waiting for transfers between devices: 0.3 us -> 8.28 us
  starting transfers between devices: 14.5 us -> 22.1 us
  Pallas kernels: 21.3 us -> 22.6 us
    all_to_all x1 -> x0, blocking collectives: 21.3 us -> none  [per_device(): lax.all_to_all(payload, ('dom', 'sub'), split_axis=0, concat_axis=0, tile...]
    all_to_all x0 -> x1, starting transfers between devices: none -> 8.35 us  [per_device(): lax.all_to_all(payload, ('dom', 'sub'), split_axis=0, concat_axis=0, tile...]
    ppermute x2, waiting for transfers between devices: 0.01 us -> 6.65 us  [exchanged(): lax.ppermute(up, 'sub', [(i, (i + 1) % count) for i in range(count)])]
    all_to_all x0 -> x1, waiting for transfers between devices: none -> 1.62 us  [per_device(): lax.all_to_all(payload, ('dom', 'sub'), split_axis=0, concat_axis=0, tile...]
    ppermute x2, starting transfers between devices: 2.54 us -> 4.11 us  [exchanged(): lax.ppermute(up, 'sub', [(i, (i + 1) % count) for i in range(count)])]
    ppermute x3 -> x1, starting transfers between devices: 2.76 us -> 1.21 us  [per_device(): lax.ppermute(pieces[k], 'dom', [(i, i ^ k) for i in range(doms)])]
    pallas_call x2, Pallas kernels: 3.14 us -> 4.37 us  [the longest x1 3.55 us: per_device(): pl.pallas_call(sums_kernel, grid=(1,), in_specs=[*[whole(small.shape)] *...]
    ppermute x2, starting transfers between devices: 9.19 us -> 8.39 us  [exchanged(): lax.ppermute(low, 'sub', [(i, (i - 1) % count) for i in range(count)])]
  transfers between devices with their start and end apart: 7 -> 6, of which waited for: 1 -> 2; matrix products, arithmetic and copies ran while one was open for 0% -> 0% of each run, Pallas kernels for 16% -> 16%
where the time goes in v4:
time: 53.8 us; the launch traced here: 53.7 us
  Pallas kernels  22.6 us (42%)
  starting transfers between devices  22.1 us (41%)
  waiting for transfers between devices  8.28 us (15%)
  between operations  0.73 us (1%)
    pallas_call x1, Pallas kernels, front(): pl.pallas_call(functools.partial(front_kernel, walls=walls), in_specs=[pl...  9.12 us
    ppermute x2, starting transfers between devices, exchanged(): lax.ppermute(low, 'sub', [(i, (i - 1) % count) for i in range(count)])  8.39 us
    all_to_all x1, starting transfers between devices, per_device(): lax.all_to_all(payload, ('dom', 'sub'), split_axis=0, concat_axis=0, tile...  8.35 us
    ppermute x2, waiting for transfers between devices, exchanged(): lax.ppermute(up, 'sub', [(i, (i + 1) % count) for i in range(count)])  6.65 us
    pallas_call x1, Pallas kernels, apply(): pl.pallas_call(functools.partial(apply_kernel, chunk=512), out_shape=[sma...  5.64 us
    ppermute x2, starting transfers between devices, exchanged(): lax.ppermute(up, 'sub', [(i, (i + 1) % count) for i in range(count)])  4.11 us
    pallas_call x1, Pallas kernels, per_device(): pl.pallas_call(sums_kernel, grid=(1,), in_specs=[*[whole(small.shape)] *...  3.55 us
    pallas_call x1, Pallas kernels, per_device(): pl.pallas_call(wall_kernel, out_shape=[shape(devices * KEPT, width)] * GR...  2.36 us
  transfers between devices with their start and end apart: 6, of which 2 were waited for; matrix products, arithmetic and copies ran while one was open for 0% of the time, Pallas kernels for 16%

profile of v4, /device:TPU:1, one launch (start us, length us, event | category | flops | bytes accessed | tf_op | source)
XLA Modules:
  0.0 53.7 jit_solution(18042066763334925712)
XLA Ops:
  0.6 0.0 copy-start.5
  0.6 0.0 copy-start.6
  0.7 9.1 %front.1 = (f32[96,128]{1,0:T(8,128)S(1)}, f32[48,256]{1,0:T(8,128)S(1)}, f32[48,256]{1,0:T(8,128)S(1)}, f32[128,2048]{1,0:T(8,128)S(1)}) custom-call(bf16[144,8192]{1,0:T(8,128)(2,1)} %refs_0_.1, bf16[144,8192]{1,0:T(8,128)(2,1)} %refs_1_.1, f32[1,8192]{1,0:T(1,128)} %bitcast.18, f32[1,8192]{1,0:T(1,128)} %bitcast.10, s32[4,8192]{1,0:T(4,128)} %conn.3, ...), custom_call_target="tpu_custom_call" | custom-call | flops 1811939328 | bytes 4718592 | tf_op jit(solution)/shard_map/front/pallas_call | solution.py:403
  9.8 2.5 %collective-permute-start = (f32[48,256]{1,0:T(8,128)S(1)}, f32[48,256]{1,0:T(8,128)S(1)}, u32[]{:S(2)}, u32[]{:S(2)}) collective-permute-start(f32[48,256]{1,0:T(8,128)S(1)} %get-tuple-element.24), channel_id=1, source_target_pairs={{0,1},{1,2},{2,3},{3,4},{4,5},{5,6},{6,7},{7,8},{8,9},{9,10},{10,1... | collective-permute-start | bytes 147464 | tf_op jit(solution)/shard_map/ppermute | solution.py:430
  12.3 4.4 %collective-permute-start.1 = (f32[48,256]{1,0:T(8,128)S(1)}, f32[48,256]{1,0:T(8,128)S(1)}, u32[]{:S(2)}, u32[]{:S(2)}) collective-permute-start(f32[48,256]{1,0:T(8,128)S(1)} %get-tuple-element.25), channel_id=1, source_target_pairs={{0,15},{1,0},{2,1},{3,2},{4,3},{5,4},{6,5},{7,6},{8,7},{9,8},{10,9... | collective-permute-start | bytes 147464 | tf_op jit(solution)/shard_map/ppermute | solution.py:431
  16.7 0.0 copy-done.5
  16.7 0.0 copy-done.6
  16.7 0.0 copy-start.1
  16.7 0.0 copy-start.2
  16.7 0.0 copy-start.3
  16.7 0.0 copy-start.4
  16.8 2.4 %walls.1 = (f32[1024,128]{1,0:T(8,128)S(1)}, f32[1024,128]{1,0:T(8,128)S(1)}) custom-call(f32[128,2048]{1,0:T(8,128)S(1)} %get-tuple-element.21.blocks, s32[1,2048]{1,0:T(1,128)S(1)} %bitcast.13, s32[1,2048]{1,0:T(1,128)S(1)} %bitcast.16), custom_call_target="tpu_custom_call" | custom-call | flops 2147483648 | bytes 2097152 | tf_op jit(solution)/shard_map/walls/pallas_call | solution.py:465
  19.1 0.0 collective-permute-done.below
  19.1 0.0 collective-permute-done.1.above
  19.1 1.2 %collective-permute-start.2 = (f32[1024,128]{1,0:T(8,128)S(1)}, f32[1024,128]{1,0:T(8,128)S(1)}, u32[]{:S(2)}, u32[]{:S(2)}) collective-permute-start(f32[1024,128]{1,0:T(8,128)S(1)} %get-tuple-element.32), channel_id=1, source_target_pairs={{0,16},{16,0},{32,48},{48,32},{64,80},{80,64},{96,112},{112,96},{1... | collective-permute-start | bytes 1572872 | tf_op jit(solution)/shard_map/ppermute | solution.py:476
  20.4 0.0 copy-done.1
  20.4 0.0 copy-done.2
  20.4 0.0 copy-done.3
  20.4 0.0 copy-done.4
  20.4 5.6 %apply.1 = (f32[48,128]{1,0:T(8,128)S(1)}, f32[48,128]{1,0:T(8,128)S(1)}, f32[48,128]{1,0:T(8,128)S(1)}, f32[3,256]{1,0:T(4,128)S(1)}, f32[3,256]{1,0:T(4,128)S(1)}) custom-call(f32[96,128]{1,0:T(8,128)S(1)} %get-tuple-element.20.field, f32[48,256]{1,0:T(8,128)S(1)} %collective-permute-done.below, f32[48,256]{1,0:T(8,128)S(1)} %collective-permute-done.1.above, ...), custom_call_target="tpu_custom_call" | custom-call | flops 805306368 | bytes 196608 | tf_op jit(solution)/shard_map/apply/pallas_call | solution.py:420
  26.0 0.0 copy-start
  26.0 0.0 collective-permute-done.2.rest_1_
  26.0 3.5 %sums.1 = f32[128,2,640]{2,1,0:T(2,128)} custom-call(f32[48,128]{1,0:T(8,128)S(1)} %get-tuple-element.28.base, f32[48,128]{1,0:T(8,128)S(1)} %get-tuple-element.29.scale, f32[48,128]{1,0:T(8,128)S(1)} %get-tuple-element.30.applied, f32[48,256]{1,0:T(8,128)S(1)} %collective-permute-done.below, f32[48,256]{1,0:T(8,128)S(1)} %collective-permute-done.1.above, ...), custom_call_target="tpu_custom_call" | custom-call | flops 786432000 | bytes 2097152 | tf_op jit(solution)/shard_map/sums/pallas_call | solution.py:487
  29.6 8.4 %all-to-all-start = ((f32[128,2,640]{2,1,0:T(2,128)}), f32[128,2,640]{2,1,0:T(2,128)S(1)}, u32[]{:S(2)}, u32[]{:S(2)}) async-start(f32[128,2,640]{2,1,0:T(2,128)} %sums.1), calls=%async_computation | async-start | bytes 1310720 | tf_op jit(solution)/shard_map/all_to_all | solution.py:502
  37.9 1.6 %collective-permute-start.3 = (f32[3,256]{1,0:T(4,128)S(1)}, f32[3,256]{1,0:T(4,128)S(1)}, u32[]{:S(2)}, u32[]{:S(2)}) collective-permute-start(f32[3,256]{1,0:T(4,128)S(1)} %get-tuple-element.36), channel_id=1, source_target_pairs={{0,1},{1,2},{2,3},{3,4},{4,5},{5,6},{6,7},{7,8},{8,9},{9,10},{10,1... | collective-permute-start | bytes 9224 | tf_op jit(solution)/shard_map/ppermute | solution.py:430
  39.5 4.0 %collective-permute-start.4 = (f32[3,256]{1,0:T(4,128)S(1)}, f32[3,256]{1,0:T(4,128)S(1)}, u32[]{:S(2)}, u32[]{:S(2)}) collective-permute-start(f32[3,256]{1,0:T(4,128)S(1)} %get-tuple-element.37), channel_id=1, source_target_pairs={{0,15},{1,0},{2,1},{3,2},{4,3},{5,4},{6,5},{7,6},{8,7},{9,8},{10,9... | collective-permute-start | bytes 9224 | tf_op jit(solution)/shard_map/ppermute | solution.py:431
  43.5 6.6 %collective-permute-done.3.below = f32[3,256]{1,0:T(4,128)S(1)} collective-permute-done((f32[3,256]{1,0:T(4,128)S(1)}, f32[3,256]{1,0:T(4,128)S(1)}, u32[]{:S(2)}, u32[]{:S(2)}) %collective-permute-start.3) | collective-permute-done | bytes 3104 | tf_op jit(solution)/shard_map/ppermute | solution.py:430
  50.1 0.0 collective-permute-done.4.above
  50.1 0.8 %adjoint.1 = f32[3,2048]{1,0:T(4,128)} custom-call(f32[48,128]{1,0:T(8,128)S(1)} %get-tuple-element.28.base, f32[48,128]{1,0:T(8,128)S(1)} %get-tuple-element.29.scale, f32[48,128]{1,0:T(8,128)S(1)} %get-tuple-element.30.applied, f32[3,256]{1,0:T(4,128)S(1)} %collective-permute-done.3.below, f32[3,256]{1,0:T(4,128)S(1)} %collective-permute-done.4.above, ...), custom_call_target="tpu_custom_call" | custom-call | flops 10000000 | bytes 100000 | tf_op jit(solution)/shard_map/adjoint/pallas_call | solution.py:504
  51.0 1.6 %all-to-all-done.got = f32[128,2,640]{2,1,0:T(2,128)S(1)} async-done(((f32[128,2,640]{2,1,0:T(2,128)}), f32[128,2,640]{2,1,0:T(2,128)S(1)}, u32[]{:S(2)}, u32[]{:S(2)}) %all-to-all-start) | async-done | bytes 655392 | tf_op jit(solution)/shard_map/all_to_all | solution.py:502
  52.6 0.0 copy-done
  52.6 1.1 %owners.1 = f32[16,128]{1,0:T(8,128)} custom-call(f32[128,2,640]{2,1,0:T(2,128)S(1)} %all-to-all-done.got, bf16[12,128]{1,0:T(8,128)(2,1)S(1)} %copy-done), custom_call_target="tpu_custom_call" | custom-call | flops 1000000 | bytes 655360 | tf_op jit(solution)/shard_map/owners/pallas_call | solution.py:510
Async XLA Ops:
  0.6 16.1 %copy-start.5 = (s32[2048,1]{0,1:T(1,128)S(1)}, s32[2048,1]{0,1:T(1,128)}, u32[]{:S(2)}) copy-start(s32[2048,1]{0,1:T(1,128)} %param.20) | copy-start | bytes 24580
  0.6 16.1 %copy-start.6 = (s32[2048]{0:T(1024)S(1)}, s32[2048]{0:T(1024)}, u32[]{:S(2)}) copy-start(s32[2048]{0:T(1024)} %param.21) | copy-start | bytes 24580
  9.8 9.3 %collective-permute-start = (f32[48,256]{1,0:T(8,128)S(1)}, f32[48,256]{1,0:T(8,128)S(1)}, u32[]{:S(2)}, u32[]{:S(2)}) collective-permute-start(f32[48,256]{1,0:T(8,128)S(1)} %get-tuple-element.24), channel_id=1, source_target_pairs={{0,1},{1,2},{2,3},{3,4},{4,5},{5,6},{6,7},{7,8},{8,9},{9,10},{10,1... | collective-permute-start | bytes 147464 | tf_op jit(solution)/shard_map/ppermute | solution.py:430
  12.3 6.8 %collective-permute-start.1 = (f32[48,256]{1,0:T(8,128)S(1)}, f32[48,256]{1,0:T(8,128)S(1)}, u32[]{:S(2)}, u32[]{:S(2)}) collective-permute-start(f32[48,256]{1,0:T(8,128)S(1)} %get-tuple-element.25), channel_id=1, source_target_pairs={{0,15},{1,0},{2,1},{3,2},{4,3},{5,4},{6,5},{7,6},{8,7},{9,8},{10,9... | collective-permute-start | bytes 147464 | tf_op jit(solution)/shard_map/ppermute | solution.py:431
  16.7 3.6 %copy-start.1 = (s32[1,1,256]{2,1,0:T(1,128)S(1)}, s32[1,1,256]{2,1,0:T(1,128)}, u32[]{:S(2)}) copy-start(s32[1,1,256]{2,1,0:T(1,128)} %param.19) | copy-start | bytes 3076
  16.7 3.6 %copy-start.2 = (s32[4,8192]{1,0:T(4,128)S(1)}, s32[4,8192]{1,0:T(4,128)}, u32[]{:S(2)}) copy-start(s32[4,8192]{1,0:T(4,128)} %conn.3) | copy-start | bytes 393220
  16.7 3.6 %copy-start.3 = (f32[8192]{0:T(1024)S(1)}, f32[8192]{0:T(1024)}, u32[]{:S(2)}) copy-start(f32[8192]{0:T(1024)} %param.17) | copy-start | bytes 98308
  16.7 3.6 %copy-start.4 = (f32[12,12]{1,0:T(8,128)S(1)}, f32[12,12]{1,0:T(8,128)}, u32[]{:S(2)}) copy-start(f32[12,12]{1,0:T(8,128)} %ref.1) | copy-start | bytes 1732
  19.1 6.9 %collective-permute-start.2 = (f32[1024,128]{1,0:T(8,128)S(1)}, f32[1024,128]{1,0:T(8,128)S(1)}, u32[]{:S(2)}, u32[]{:S(2)}) collective-permute-start(f32[1024,128]{1,0:T(8,128)S(1)} %get-tuple-element.32), channel_id=1, source_target_pairs={{0,16},{16,0},{32,48},{48,32},{64,80},{80,64},{96,112},{112,96},{1... | collective-permute-start | bytes 1572872 | tf_op jit(solution)/shard_map/ppermute | solution.py:476
  26.0 26.6 %copy-start = (bf16[12,128]{1,0:T(8,128)(2,1)S(1)}, bf16[12,128]{1,0:T(8,128)(2,1)}, u32[]{:S(2)}) copy-start(bf16[12,128]{1,0:T(8,128)(2,1)} %w_adjoint.1) | copy-start | bytes 9220
  29.6 23.0 %all-to-all-start = ((f32[128,2,640]{2,1,0:T(2,128)}), f32[128,2,640]{2,1,0:T(2,128)S(1)}, u32[]{:S(2)}, u32[]{:S(2)}) async-start(f32[128,2,640]{2,1,0:T(2,128)} %sums.1), calls=%async_computation | async-start | bytes 1310720 | tf_op jit(solution)/shard_map/all_to_all | solution.py:502
  37.9 12.2 %collective-permute-start.3 = (f32[3,256]{1,0:T(4,128)S(1)}, f32[3,256]{1,0:T(4,128)S(1)}, u32[]{:S(2)}, u32[]{:S(2)}) collective-permute-start(f32[3,256]{1,0:T(4,128)S(1)} %get-tuple-element.36), channel_id=1, source_target_pairs={{0,1},{1,2},{2,3},{3,4},{4,5},{5,6},{6,7},{7,8},{8,9},{9,10},{10,1... | collective-permute-start | bytes 9224 | tf_op jit(solution)/shard_map/ppermute | solution.py:430
  39.5 10.6 %collective-permute-start.4 = (f32[3,256]{1,0:T(4,128)S(1)}, f32[3,256]{1,0:T(4,128)S(1)}, u32[]{:S(2)}, u32[]{:S(2)}) collective-permute-start(f32[3,256]{1,0:T(4,128)S(1)} %get-tuple-element.37), channel_id=1, source_target_pairs={{0,15},{1,0},{2,1},{3,2},{4,3},{5,4},{6,5},{7,6},{8,7},{9,8},{10,9... | collective-permute-start | bytes 9224 | tf_op jit(solution)/shard_map/ppermute | solution.py:431

commit v5 on v4

--- a/solution.py
+++ b/solution.py
@@ -121,10 +121,10 @@
 
 
 def front_kernel(*refs, walls):
-    count = (len(refs) - 5) // 2
-    sources, (field, up, low, blocks), held = refs[:count], refs[count : count + 4], refs[count + 4 : -1]
-    sems = refs[-1]
-    traces, states, jac, stiff, conn, w_trace, w_state, w_node, w_block, perm, ref, owner, patch = held
+    count = (len(refs) - 6) // 2
+    sources, w_node, (field, up, low, wall_product) = refs[:count], refs[count], refs[count + 1 : count + 5]
+    held, sems = refs[count + 5 : -1], refs[-1]
+    traces, states, jac, stiff, conn, w_trace, w_state, perm, ref, owner, patch = held
     cuts = [0, walls // 4, *range(walls, traces.shape[1] + 1, walls)]
     spans = [slice(p, q) for p, q in zip(cuts, cuts[1:])]
     copies = []
@@ -138,18 +138,19 @@
         copies.append(copy)
         return copy
 
-    weights = [fetch(k) for k in (5, 6, 7, 8)]
-    first = [fetch(0, spans[0]), fetch(1, spans[0]), fetch(2)]
+    weights = [fetch(5)]
+    first = [fetch(0, spans[0])]
+    weights.append(fetch(6))
+    first += [fetch(1, spans[0]), fetch(2)]
     small = [fetch(k) for k in (3, 4)]
     later = [[fetch(0, span), fetch(1, span)] for span in spans[1:]]
-    last = [fetch(k) for k in (9, 10, 11, 12)]
-    for copy in weights:
-        copy.wait()
+    last = [fetch(k) for k in (7, 8, 9, 10)]
+    weights[0].wait()
     trace_t = w_trace[...].astype(f32).T.astype(bf16)
+    weights[1].wait()
     state_t = w_state[...].astype(f32).T.astype(bf16)
     pad = jnp.zeros((4, w_node.shape[1]), f32)
     node_t = jnp.concatenate([w_node[...].astype(f32), pad], axis=0).astype(bf16)
-    block_t = w_block[...].astype(f32).T.astype(bf16)
     cut = FIELDS * HIS
     sums = [jnp.zeros((LANES, 2 * (cut + HIS)), f32) for _ in range(4)]
     for s, span in enumerate(spans):
@@ -160,7 +161,7 @@
         product = (jac[:, span] * upsilon * tangent).astype(bf16)
         terms = mxu(node_t, product, NN)
         if s < 2:
-            blocks[:, span] = mxu(block_t, product, NN)
+            wall_product[:, span] = product
         if s == 0:
             for copy in small:
                 copy.wait()
@@ -196,11 +197,12 @@
     return lax.axis_index("dom") % GROUP
 
 
-def wall_kernel(blocks, owner, patch, *sums):
+def wall_kernel(product, w_block, owner, patch, *sums):
     rows = sums[0].shape[0]
     owners = rows // KEPT
     slot = (patch[...] // KEPT ^ group_place()) * rows + patch[...] % KEPT * owners + owner[...]
-    top, rest = halves(blocks[...])
+    blocks = mxu(w_block[...].astype(f32).T.astype(bf16), product[...], NN)
+    top, rest = halves(blocks)
     both = jnp.concatenate([top, rest], axis=0).astype(bf16)
     for k in range(GROUP):
         out = mxu(one_hot(slot - k * rows, rows), both, NT)
@@ -265,7 +267,8 @@
 
     half = conn.shape[1] // 2
     total = jnp.zeros((cut, LANES), f32)
-    for start in range(0, half, chunk):
+
+    def prepare(start):
         first = slice(start, start + chunk)
         second = slice(half + start, half + start + chunk)
         slots = jnp.concatenate([conn[:, first], conn[:, second]], axis=0)
@@ -276,10 +279,16 @@
         in_first = lax.broadcasted_iota(jnp.int32, (8, chunk), 0) < 4
         weight = jnp.where(in_first, stiff[:, first], stiff[:, second])
         pushed = pushed * jnp.concatenate([weight] * FIELDS, axis=0)
-        top, rest = halves(pushed)
+        return slots, halves(pushed)
+
+    ready = prepare(0)
+    for start in range(0, half, chunk):
+        slots, parts = ready
+        if start + chunk < half:
+            ready = prepare(start + chunk)
         high, lane = slots >> 7, slots & (LANES - 1)
         for row in range(8):
-            rows = [x[c * 8 + row : c * 8 + row + 1] for x in (top, rest) for c in range(FIELDS)]
+            rows = [x[c * 8 + row : c * 8 + row + 1] for x in parts for c in range(FIELDS)]
             spread = placed(high[row : row + 1], rows)
             out = mxu(spread, one_hot(lane[row : row + 1], LANES), NT)
             total += out[:cut] + out[cut:]
@@ -288,9 +297,9 @@
     low[...] = reorder(rim_rows(total, 0), perm[...], NN)
 
 
-def patch_sums(values, targets, owners):
+def patch_parts(values, targets, owners):
     parts = [halves(v) for v in values]
-    total = jnp.zeros((owners, 24 * PATCH_DEV), f32)
+    out = []
     for k, target in enumerate(targets):
         rows = [
             parts[c][p][4 * k + a : 4 * k + a + 1]
@@ -298,9 +307,8 @@
             for c in range(FIELDS)
             for a in range(4)
         ]
-        spread = placed(target % PATCH_DEV, rows)
-        total += mxu(one_hot(target // PATCH_DEV, owners), spread, NT)
-    return total[:, : 12 * PATCH_DEV] + total[:, 12 * PATCH_DEV :]
+        out.append((one_hot(target // PATCH_DEV, owners), placed(target % PATCH_DEV, rows)))
+    return out
 
 
 def sums_kernel(base, scale, applied, below, above, conn, owner, patch, perm, *rest):
@@ -308,22 +316,26 @@
     owners = payload.shape[0]
     change = scale[...] * applied[...]
     psi = base[...] - change
-    half = conn.shape[1] // 2
-    slots = jnp.concatenate([conn[:, :half], conn[:, half:]], axis=0)
+    walls = owner.shape[1]
+    half = walls // 2
+    slots = jnp.concatenate([conn[:, :half], conn[:, half:walls]], axis=0)
     target = owner[...] * PATCH_DEV + patch[...]
     values = looked_up(all_lines(psi), slots)
-    total = patch_sums(values, [target[:, :half], target[:, half:]], owners)
+    terms = patch_parts(values, [target[:, :half], target[:, half:]], owners)
 
     place = lax.axis_index("sub")
     last = lax.axis_size("sub") - 1
     lower = reorder(rim_rows(-change, 0), perm[...], NN)
     lower = jnp.where(place == 0, 0.0, lower)
     slots, targets = read_message(below)
-    total += patch_sums(looked_up(rim_lines(lower, HIS - 2), slots), targets, owners)
+    terms += patch_parts(looked_up(rim_lines(lower, HIS - 2), slots), targets, owners)
     upper = reorder(rim_rows(-change, HIS - 2), above[6:7].astype(jnp.int32), NT)
     upper = jnp.where(place == last, 0.0, upper)
     slots, targets = read_message(above)
-    total += patch_sums(looked_up(rim_lines(upper, 0), slots), targets, owners)
+    terms += patch_parts(looked_up(rim_lines(upper, 0), slots), targets, owners)
+    left, right = (jnp.concatenate(x, axis=1) for x in zip(*terms))
+    total = mxu(left, right, NT)
+    total = total[:, : 12 * PATCH_DEV] + total[:, 12 * PATCH_DEV :]
 
     total = jnp.concatenate([total, jnp.zeros((owners, 4 * PATCH_DEV), f32)], axis=1)
     kept = pieces[0][...]
@@ -386,23 +398,21 @@
     )
 
 
-def whole(shape):
-    return pl.BlockSpec(shape, lambda s: (0,) * len(shape))
-
-
 def shape(*dims):
     return jax.ShapeDtypeStruct(dims, f32)
 
 
-def front(walls, *fetched):
+def front(walls, node_t, *fetched):
     trace, elements = fetched[0].shape
-    quad, width = fetched[8].shape
+    quad = fetched[5].shape[1]
     message = shape(8 + 5 * PIECES, RIM)
-    outs = [shape(2 * FIELDS * HIS, LANES), message, message, shape(width, walls)]
+    product = jax.ShapeDtypeStruct((quad, walls), bf16)
+    outs = [shape(2 * FIELDS * HIS, LANES), message, message, product]
     copies = len(fetched) + 2 * (elements // walls)
     return pl.pallas_call(
         functools.partial(front_kernel, walls=walls),
-        in_specs=[pl.BlockSpec(memory_space=pl.ANY)] * len(fetched),
+        in_specs=[pl.BlockSpec(memory_space=pl.ANY)] * len(fetched)
+        + [pl.BlockSpec(memory_space=pltpu.VMEM)],
         out_shape=outs,
         scratch_shapes=[
             *(pltpu.VMEM(x.shape, x.dtype) for x in fetched),
@@ -410,7 +420,7 @@
         ],
         name="front",
         **params(4 * elements * trace * quad, 4 * elements * trace, FRONT_VMEM),
-    )(*(pltpu.with_memory_space_constraint(x, pltpu.HBM) for x in fetched))
+    )(*(pltpu.with_memory_space_constraint(x, pltpu.HBM) for x in fetched), node_t)
 
 
 def apply(field, below, above, connect, stiff, perm, stiff_ref):
@@ -456,9 +466,9 @@
     owner = wall_owner.reshape(1, -1)
     patch = wall_patch.reshape(1, -1)
     perm = shared_perm.reshape(1, -1)
-    field, up, low, blocks = front(
-        walls, adjoint_traces, primal_traces, jac, stiff, connect,
-        w_trace, w_state, w_node.T, w_block, perm, stiff_ref, owner, patch,
+    field, up, low, product = front(
+        walls, w_node.T, adjoint_traces, primal_traces, jac, stiff, connect,
+        w_trace, w_state, perm, stiff_ref, owner, patch,
     )
     below, above = exchanged(up, low)
 
@@ -467,7 +477,7 @@
         out_shape=[shape(devices * KEPT, width)] * GROUP,
         name="walls",
         **params(4 * walls * width * devices * PATCH_DEV, 8 * walls * width),
-    )(blocks, owner, patch)
+    )(product, w_block, owner, patch)
     *pieces, below, above = lax.optimization_barrier((*pieces, below, above))
     doms = lax.axis_size("dom")
     pieces = [
@@ -482,17 +492,9 @@
     base, scale, applied, up, low = apply(
         field, below, above, connect, stiff, perm, stiff_ref
     )
-    conn_spec = pl.BlockSpec((4, walls), lambda s: (0, 0))
     payload = shape(devices, 2, ROWS // 2 * LANES)
     payload = pl.pallas_call(
         sums_kernel,
-        grid=(1,),
-        in_specs=[
-            *[whole(small.shape)] * 3, *[whole(below.shape)] * 2, conn_spec,
-            whole(owner.shape), whole(patch.shape), whole(perm.shape),
-            *[whole(pieces[0].shape)] * GROUP,
-        ],
-        out_specs=whole(payload.shape),
         out_shape=payload,
         name="sums",
         **params(3000 * walls * LANES, 8 * devices * PATCH_DEV * width),

time: 53.8 us -> 53.6 us (level)
  local copies, waits for them, and re-layouts: 0.03 us -> 0.74 us
  Pallas kernels: 22.6 us -> 22 us
    unnamed x14 -> x18, local copies, waits for them, and re-layouts: 0.03 us -> 0.74 us
  transfers between devices with their start and end apart: 6 -> 6, of which waited for: 2 -> 2; matrix products, arithmetic and copies ran while one was open for 0% -> 0% of each run, Pallas kernels for 16% -> 17%
where the time goes in v5:
time: 53.6 us; the launch traced here: 53.4 us
  Pallas kernels  22 us (41%)
  starting transfers between devices  21.7 us (40%)
  waiting for transfers between devices  8.28 us (15%)
  local copies, waits for them, and re-layouts  0.74 us (1%)
  between operations  0.73 us (1%)
    pallas_call x1, Pallas kernels, front(): pl.pallas_call(functools.partial(front_kernel, walls=walls), in_specs=[pl...  8.78 us
    ppermute x2, starting transfers between devices, exchanged(): lax.ppermute(low, 'sub', [(i, (i - 1) % count) for i in range(count)])  8.39 us
    all_to_all x1, starting transfers between devices, per_device(): lax.all_to_all(payload, ('dom', 'sub'), split_axis=0, concat_axis=0, tile...  7.98 us
    ppermute x2, waiting for transfers between devices, exchanged(): lax.ppermute(up, 'sub', [(i, (i + 1) % count) for i in range(count)])  6.65 us
    pallas_call x1, Pallas kernels, apply(): pl.pallas_call(functools.partial(apply_kernel, chunk=512), out_shape=[sma...  5.32 us
    ppermute x2, starting transfers between devices, exchanged(): lax.ppermute(up, 'sub', [(i, (i + 1) % count) for i in range(count)])  4.11 us
    pallas_call x1, Pallas kernels, per_device(): pl.pallas_call(sums_kernel, out_shape=payload, name='sums', **params(3000...  3.28 us
    pallas_call x1, Pallas kernels, per_device(): pl.pallas_call(wall_kernel, out_shape=[shape(devices * KEPT, width)] * GR...  2.7 us
  transfers between devices with their start and end apart: 6, of which 2 were waited for; matrix products, arithmetic and copies ran while one was open for 0% of the time, Pallas kernels for 17%

profile of v5, /device:TPU:1, one launch (start us, length us, event | category | flops | bytes accessed | tf_op | source)
XLA Modules:
  0.0 53.4 jit_solution(4451137875574231744)
XLA Ops:
  0.6 0.0 copy-start.5
  0.6 0.7 %copy-done.5 = bf16[384,12]{0,1:T(8,128)(2,1)S(1)} copy-done((bf16[384,12]{0,1:T(8,128)(2,1)S(1)}, bf16[384,12]{0,1:T(8,128)(2,1)}, u32[]{:S(2)}) %copy-start.5) | copy-done | bytes 9240
  1.3 0.0 copy-start.3
  1.3 8.8 %front.1 = (f32[96,128]{1,0:T(8,128)S(1)}, f32[48,256]{1,0:T(8,128)S(1)}, f32[48,256]{1,0:T(8,128)S(1)}, bf16[384,2048]{1,0:T(8,128)(2,1)S(1)}) custom-call(bf16[144,8192]{1,0:T(8,128)(2,1)} %refs_0_.1, bf16[144,8192]{1,0:T(8,128)(2,1)} %refs_1_.1, f32[1,8192]{1,0:T(1,128)} %bitcast.19, f32[1,8192]{1,0:T(1,128)} %bitcast.10, s32[4,8192]{1,0:T(4,128)} %conn.3, ...), custom_call_target="tpu_custom_call" | custom-call | flops 1811939328 | bytes 4718592 | tf_op jit(solution)/shard_map/front/pallas_call | solution.py:412
  10.1 2.5 %collective-permute-start = (f32[48,256]{1,0:T(8,128)S(1)}, f32[48,256]{1,0:T(8,128)S(1)}, u32[]{:S(2)}, u32[]{:S(2)}) collective-permute-start(f32[48,256]{1,0:T(8,128)S(1)} %get-tuple-element.24), channel_id=1, source_target_pairs={{0,1},{1,2},{2,3},{3,4},{4,5},{5,6},{6,7},{7,8},{8,9},{9,10},{10,1... | collective-permute-start | bytes 147464 | tf_op jit(solution)/shard_map/ppermute | solution.py:440
  12.7 4.4 %collective-permute-start.1 = (f32[48,256]{1,0:T(8,128)S(1)}, f32[48,256]{1,0:T(8,128)S(1)}, u32[]{:S(2)}, u32[]{:S(2)}) collective-permute-start(f32[48,256]{1,0:T(8,128)S(1)} %get-tuple-element.25), channel_id=1, source_target_pairs={{0,15},{1,0},{2,1},{3,2},{4,3},{5,4},{6,5},{7,6},{8,7},{9,8},{10,9... | collective-permute-start | bytes 147464 | tf_op jit(solution)/shard_map/ppermute | solution.py:441
  17.1 0.0 copy-done.3
  17.1 0.0 copy-done.7
  17.1 0.0 copy-done.8
  17.1 0.0 copy-start.2
  17.1 0.0 copy-start.4
  17.1 0.0 copy-start.6
  17.1 2.7 %walls.1 = (f32[1024,128]{1,0:T(8,128)S(1)}, f32[1024,128]{1,0:T(8,128)S(1)}) custom-call(bf16[384,2048]{1,0:T(8,128)(2,1)S(1)} %get-tuple-element.21.product, bf16[384,128]{1,0:T(8,128)(2,1)S(1)} %copy-done.3, s32[1,2048]{1,0:T(1,128)S(1)} %bitcast.14, s32[1,2048]{1,0:T(1,128)S(1)} %bitcast.17), custom_call_target="tpu_custom_call" | custom-call | flops 2147483648 | bytes 2097152 | tf_op jit(solution)/shard_map/walls/pallas_call | solution.py:475
  19.8 0.0 collective-permute-done.below
  19.8 0.0 collective-permute-done.1.above
  19.9 1.2 %collective-permute-start.2 = (f32[1024,128]{1,0:T(8,128)S(1)}, f32[1024,128]{1,0:T(8,128)S(1)}, u32[]{:S(2)}, u32[]{:S(2)}) collective-permute-start(f32[1024,128]{1,0:T(8,128)S(1)} %get-tuple-element.32), channel_id=1, source_target_pairs={{0,16},{16,0},{32,48},{48,32},{64,80},{80,64},{96,112},{112,96},{1... | collective-permute-start | bytes 1572872 | tf_op jit(solution)/shard_map/ppermute | solution.py:486
  21.1 0.0 copy-done.1
  21.1 0.0 copy-done.2
  21.1 0.0 copy-done.4
  21.1 0.0 copy-done.6
  21.1 5.3 %apply.1 = (f32[48,128]{1,0:T(8,128)S(1)}, f32[48,128]{1,0:T(8,128)S(1)}, f32[48,128]{1,0:T(8,128)S(1)}, f32[3,256]{1,0:T(4,128)S(1)}, f32[3,256]{1,0:T(4,128)S(1)}) custom-call(f32[96,128]{1,0:T(8,128)S(1)} %get-tuple-element.20.field, f32[48,256]{1,0:T(8,128)S(1)} %collective-permute-done.below, f32[48,256]{1,0:T(8,128)S(1)} %collective-permute-done.1.above, ...), custom_call_target="tpu_custom_call" | custom-call | flops 805306368 | bytes 196608 | tf_op jit(solution)/shard_map/apply/pallas_call | solution.py:430
  26.4 0.0 collective-permute-done.2.rest_1_
  26.4 3.3 %sums.1 = f32[128,2,640]{2,1,0:T(2,128)} custom-call(f32[48,128]{1,0:T(8,128)S(1)} %get-tuple-element.28.base, f32[48,128]{1,0:T(8,128)S(1)} %get-tuple-element.29.scale, f32[48,128]{1,0:T(8,128)S(1)} %get-tuple-element.30.applied, f32[48,256]{1,0:T(8,128)S(1)} %collective-permute-done.below, f32[48,256]{1,0:T(8,128)S(1)} %collective-permute-done.1.above, ...), custom_call_target="tpu_custom_call" | custom-call | flops 786432000 | bytes 2097152 | tf_op jit(solution)/shard_map/sums/pallas_call | solution.py:496
  29.7 8.0 %all-to-all-start = ((f32[128,2,640]{2,1,0:T(2,128)}), f32[128,2,640]{2,1,0:T(2,128)S(1)}, u32[]{:S(2)}, u32[]{:S(2)}) async-start(f32[128,2,640]{2,1,0:T(2,128)} %sums.1), calls=%async_computation | async-start | bytes 1310720 | tf_op jit(solution)/shard_map/all_to_all | solution.py:504
  37.7 1.6 %collective-permute-start.3 = (f32[3,256]{1,0:T(4,128)S(1)}, f32[3,256]{1,0:T(4,128)S(1)}, u32[]{:S(2)}, u32[]{:S(2)}) collective-permute-start(f32[3,256]{1,0:T(4,128)S(1)} %get-tuple-element.36), channel_id=1, source_target_pairs={{0,1},{1,2},{2,3},{3,4},{4,5},{5,6},{6,7},{7,8},{8,9},{9,10},{10,1... | collective-permute-start | bytes 9224 | tf_op jit(solution)/shard_map/ppermute | solution.py:440
  39.3 4.0 %collective-permute-start.4 = (f32[3,256]{1,0:T(4,128)S(1)}, f32[3,256]{1,0:T(4,128)S(1)}, u32[]{:S(2)}, u32[]{:S(2)}) collective-permute-start(f32[3,256]{1,0:T(4,128)S(1)} %get-tuple-element.37), channel_id=1, source_target_pairs={{0,15},{1,0},{2,1},{3,2},{4,3},{5,4},{6,5},{7,6},{8,7},{9,8},{10,9... | collective-permute-start | bytes 9224 | tf_op jit(solution)/shard_map/ppermute | solution.py:441
  43.3 6.6 %collective-permute-done.3.below = f32[3,256]{1,0:T(4,128)S(1)} collective-permute-done((f32[3,256]{1,0:T(4,128)S(1)}, f32[3,256]{1,0:T(4,128)S(1)}, u32[]{:S(2)}, u32[]{:S(2)}) %collective-permute-start.3) | collective-permute-done | bytes 3104 | tf_op jit(solution)/shard_map/ppermute | solution.py:440
  49.9 0.0 collective-permute-done.4.above
  49.9 0.8 %adjoint.1 = f32[3,2048]{1,0:T(4,128)} custom-call(f32[48,128]{1,0:T(8,128)S(1)} %get-tuple-element.28.base, f32[48,128]{1,0:T(8,128)S(1)} %get-tuple-element.29.scale, f32[48,128]{1,0:T(8,128)S(1)} %get-tuple-element.30.applied, f32[3,256]{1,0:T(4,128)S(1)} %collective-permute-done.3.below, f32[3,256]{1,0:T(4,128)S(1)} %collective-permute-done.4.above, ...), custom_call_target="tpu_custom_call" | custom-call | flops 10000000 | bytes 100000 | tf_op jit(solution)/shard_map/adjoint/pallas_call | solution.py:506
  50.7 1.6 %all-to-all-done.got = f32[128,2,640]{2,1,0:T(2,128)S(1)} async-done(((f32[128,2,640]{2,1,0:T(2,128)}), f32[128,2,640]{2,1,0:T(2,128)S(1)}, u32[]{:S(2)}, u32[]{:S(2)}) %all-to-all-start) | async-done | bytes 655392 | tf_op jit(solution)/shard_map/all_to_all | solution.py:504
  52.3 0.0 copy-done
  52.3 1.1 %owners.1 = f32[16,128]{1,0:T(8,128)} custom-call(f32[128,2,640]{2,1,0:T(2,128)S(1)} %all-to-all-done.got, bf16[12,128]{1,0:T(8,128)(2,1)S(1)} %copy-done), custom_call_target="tpu_custom_call" | custom-call | flops 1000000 | bytes 655360 | tf_op jit(solution)/shard_map/owners/pallas_call | solution.py:512
  (4 shorter events, 0.0 us)
Async XLA Ops:
  0.6 0.7 %copy-start.5 = (bf16[384,12]{0,1:T(8,128)(2,1)S(1)}, bf16[384,12]{0,1:T(8,128)(2,1)}, u32[]{:S(2)}) copy-start(bf16[384,12]{0,1:T(8,128)(2,1)} %param.24) | copy-start | bytes 27652
  1.3 15.7 %copy-start.3 = (bf16[384,128]{1,0:T(8,128)(2,1)S(1)}, bf16[384,128]{1,0:T(8,128)(2,1)}, u32[]{:S(2)}) copy-start(bf16[384,128]{1,0:T(8,128)(2,1)} %w_block.1) | copy-start | bytes 294916
  1.3 15.7 %copy-start.7 = (s32[2048,1]{0,1:T(1,128)S(1)}, s32[2048,1]{0,1:T(1,128)}, u32[]{:S(2)}) copy-start(s32[2048,1]{0,1:T(1,128)} %param.20) | copy-start | bytes 24580
  1.3 15.7 %copy-start.8 = (s32[2048]{0:T(1024)S(1)}, s32[2048]{0:T(1024)}, u32[]{:S(2)}) copy-start(s32[2048]{0:T(1024)} %param.21) | copy-start | bytes 24580
  10.1 9.7 %collective-permute-start = (f32[48,256]{1,0:T(8,128)S(1)}, f32[48,256]{1,0:T(8,128)S(1)}, u32[]{:S(2)}, u32[]{:S(2)}) collective-permute-start(f32[48,256]{1,0:T(8,128)S(1)} %get-tuple-element.24), channel_id=1, source_target_pairs={{0,1},{1,2},{2,3},{3,4},{4,5},{5,6},{6,7},{7,8},{8,9},{9,10},{10,1... | collective-permute-start | bytes 147464 | tf_op jit(solution)/shard_map/ppermute | solution.py:440
  12.7 7.2 %collective-permute-start.1 = (f32[48,256]{1,0:T(8,128)S(1)}, f32[48,256]{1,0:T(8,128)S(1)}, u32[]{:S(2)}, u32[]{:S(2)}) collective-permute-start(f32[48,256]{1,0:T(8,128)S(1)} %get-tuple-element.25), channel_id=1, source_target_pairs={{0,15},{1,0},{2,1},{3,2},{4,3},{5,4},{6,5},{7,6},{8,7},{9,8},{10,9... | collective-permute-start | bytes 147464 | tf_op jit(solution)/shard_map/ppermute | solution.py:441
  17.1 4.0 %copy-start.1 = (s32[1,1,256]{2,1,0:T(1,128)S(1)}, s32[1,1,256]{2,1,0:T(1,128)}, u32[]{:S(2)}) copy-start(s32[1,1,256]{2,1,0:T(1,128)} %param.19) | copy-start | bytes 3076
  17.1 4.0 %copy-start.2 = (s32[4,8192]{1,0:T(4,128)S(1)}, s32[4,8192]{1,0:T(4,128)}, u32[]{:S(2)}) copy-start(s32[4,8192]{1,0:T(4,128)} %conn.3) | copy-start | bytes 393220
  17.1 4.0 %copy-start.4 = (f32[8192]{0:T(1024)S(1)}, f32[8192]{0:T(1024)}, u32[]{:S(2)}) copy-start(f32[8192]{0:T(1024)} %param.17) | copy-start | bytes 98308
  17.1 4.0 %copy-start.6 = (f32[12,12]{1,0:T(8,128)S(1)}, f32[12,12]{1,0:T(8,128)}, u32[]{:S(2)}) copy-start(f32[12,12]{1,0:T(8,128)} %ref.1) | copy-start | bytes 1732
  19.9 6.6 %collective-permute-start.2 = (f32[1024,128]{1,0:T(8,128)S(1)}, f32[1024,128]{1,0:T(8,128)S(1)}, u32[]{:S(2)}, u32[]{:S(2)}) collective-permute-start(f32[1024,128]{1,0:T(8,128)S(1)} %get-tuple-element.32), channel_id=1, source_target_pairs={{0,16},{16,0},{32,48},{48,32},{64,80},{80,64},{96,112},{112,96},{1... | collective-permute-start | bytes 1572872 | tf_op jit(solution)/shard_map/ppermute | solution.py:486
  26.4 25.9 %copy-start = (bf16[12,128]{1,0:T(8,128)(2,1)S(1)}, bf16[12,128]{1,0:T(8,128)(2,1)}, u32[]{:S(2)}) copy-start(bf16[12,128]{1,0:T(8,128)(2,1)} %w_adjoint.1) | copy-start | bytes 9220
  29.7 22.6 %all-to-all-start = ((f32[128,2,640]{2,1,0:T(2,128)}), f32[128,2,640]{2,1,0:T(2,128)S(1)}, u32[]{:S(2)}, u32[]{:S(2)}) async-start(f32[128,2,640]{2,1,0:T(2,128)} %sums.1), calls=%async_computation | async-start | bytes 1310720 | tf_op jit(solution)/shard_map/all_to_all | solution.py:504
  37.7 12.2 %collective-permute-start.3 = (f32[3,256]{1,0:T(4,128)S(1)}, f32[3,256]{1,0:T(4,128)S(1)}, u32[]{:S(2)}, u32[]{:S(2)}) collective-permute-start(f32[3,256]{1,0:T(4,128)S(1)} %get-tuple-element.36), channel_id=1, source_target_pairs={{0,1},{1,2},{2,3},{3,4},{4,5},{5,6},{6,7},{7,8},{8,9},{9,10},{10,1... | collective-permute-start | bytes 9224 | tf_op jit(solution)/shard_map/ppermute | solution.py:440
  39.3 10.6 %collective-permute-start.4 = (f32[3,256]{1,0:T(4,128)S(1)}, f32[3,256]{1,0:T(4,128)S(1)}, u32[]{:S(2)}, u32[]{:S(2)}) collective-permute-start(f32[3,256]{1,0:T(4,128)S(1)} %get-tuple-element.37), channel_id=1, source_target_pairs={{0,15},{1,0},{2,1},{3,2},{4,3},{5,4},{6,5},{7,6},{8,7},{9,8},{10,9... | collective-permute-start | bytes 9224 | tf_op jit(solution)/shard_map/ppermute | solution.py:441
